TPU v7x, 512 devices: a whole 4x4x16 slice. The times are simulated.
512 devices in a mesh: row: 128 (over y, z, x_lo), rep: 4 (over x_hi, core).
Axes of the slice: x: 4 (x_hi: 2, x_lo: 2; x = x_hi * 2 + x_lo), y: 4, z: 16, core: 2. Of those that a mesh axis runs over, the one named last changes fastest.
Arguments:
- features: bfloat16 [65536, 128], P(('row', 'rep')), may hold values from -6 to 6
- weight: bfloat16 [128, 256], replicated, may hold values from -0.5 to 0.5
- upstream: bfloat16 [65536, 256], P(('row', 'rep')), may hold values from -6 to 6
- tile_owners: int32 [512, 4, 4], P('row', 'rep'), may hold values from 0 to 127
- tile_counts: int32 [512, 4], P('row', 'rep'), may hold values from 1 to 4, 10 in all within a row
- tile_values: bfloat16 [512, 4, 4, 128, 128], P('row', 'rep'), may hold values from -0.15625 to 0.15625
Outputs:
- hidden: bfloat16 [65536, 256], P(('row', 'rep'))
- grad_weight: float32 [128, 256], replicated
- grad_features: float32 [65536, 128], P(('row', 'rep'))
All inputs are finite; a program needn't handle non-finite values. No bound on the sum of `tile_counts` on one device may be relied on, other than what follows from the above.
Results may differ from a plain program's by a relative error of at most 0.0057.
Values may be sent and summed in bfloat16 or wider, within the bound.
No kernel may reach another device: no remote copies, remote signals or barrier semaphores. Data moves between devices by JAX's collectives and lax.ppermute only.
A program may use at most 128 MiB of HBM per device.

v0:
```python
import jax
import jax.numpy as jnp
from jax import lax
from jax.sharding import PartitionSpec as P


def forward_slots(values, owners, active, sources):
    picked = jnp.where(active[:, :, None, None], sources[owners], jnp.zeros((), jnp.bfloat16))
    return jnp.einsum("btij,btjf->bif", values, picked, preferred_element_type=jnp.float32)


def backward_slots(values, owners, active, back_rows, running):
    parts = jnp.einsum("btji,bjf->btif", values, back_rows, preferred_element_type=jnp.float32)
    parts = jnp.where(active[:, :, None, None], parts, jnp.zeros((), jnp.float32))
    return running.at[owners.reshape(-1)].add(parts.reshape(-1, parts.shape[2], parts.shape[3]))


def body(features, weight, upstream, tile_owners, tile_counts, tile_values):
    tile_size, width = features.shape
    row_count = lax.axis_size("row")
    owners = tile_owners[:, 0, :]
    counts = tile_counts[:, 0]
    values = tile_values[:, 0]
    block_count, slot_count = owners.shape
    active = jnp.arange(slot_count, dtype=jnp.int32)[None, :] < counts[:, None]
    gathered = lax.all_gather(features, "row", axis=0, tiled=True)
    sources = gathered.reshape(row_count, tile_size, width)
    partial_value = forward_slots(values, owners, active, sources)
    totals = lax.psum(partial_value, "rep")
    aggregated = totals.astype(jnp.bfloat16).reshape(block_count * tile_size, width)
    pre_act = jnp.dot(aggregated, weight, preferred_element_type=jnp.float32)
    own_start = lax.axis_index("rep") * tile_size
    hidden_all = jax.nn.gelu(pre_act).astype(jnp.bfloat16)
    hidden = lax.dynamic_slice_in_dim(hidden_all, own_start, tile_size, 0)
    upstream_all = lax.all_gather(upstream, "rep", axis=0, tiled=True)
    unused_value, pullback = jax.vjp(jax.nn.gelu, pre_act)
    slope = pullback(upstream_all.astype(jnp.float32))[0].astype(jnp.bfloat16)
    grad_weight = lax.psum(jnp.dot(aggregated.T, slope, preferred_element_type=jnp.float32), "row")
    back_flat = jnp.dot(slope, weight.T, preferred_element_type=jnp.float32).astype(jnp.bfloat16)
    back_rows = back_flat.reshape(block_count, tile_size, width)
    empty_term = jnp.zeros((row_count, tile_size, width), jnp.float32)
    term = backward_slots(values, owners, active, back_rows, empty_term)
    received = lax.all_to_all(term, "row", split_axis=0, concat_axis=0, tiled=True)
    grad_features = jnp.sum(received, axis=0)
    return (hidden, grad_weight, grad_features)


def solution(mesh):
    in_specs = (
        P(("row", "rep"), None),
        P(),
        P(("row", "rep"), None),
        P("row", "rep", None),
        P("row", "rep"),
        P("row", "rep", None, None, None),
    )
    out_specs = (P(("row", "rep"), None), P(), P(("row", "rep"), None))
    return jax.shard_map(body, mesh=mesh, in_specs=in_specs, out_specs=out_specs, check_vma=False)
```

profile of v0, /device:TPU:2, one launch (start us, length us, event | category | flops | bytes accessed | tf_op | source)
XLA Modules:
  0.0 1757.7 jit_solution(8851435798862854127)
XLA Ops:
  7.2 0.0 copy-start
  7.2 0.0 all-gather.2.cloned.1.call-start
  7.2 0.7 all-gather.2.cloned.1.call-update
  7.9 0.5 broadcast.105
  8.4 1.3 reduce.3
  9.8 0.1 reshape_squeeze.3
  9.9 0.7 compare_select_fusion
  10.5 0.1 reshape.102
  10.6 7.5 all_gather.7
  18.1 0.7 iota_compare_fusion
  18.9 589.4 %all-gather.2.cloned.1.call-done = bf16[16384,128]{1,0:T(8,128)(2,1)} async-done(((bf16[128,128]{1,0:T(8,128)(2,1)}), bf16[16384,128]{1,0:T(8,128)(2,1)}) %all-gather.2.cloned.1.call-update) | async-done | bytes 4194320 | tf_op jit(solution)/shard_map/all_gather | solution.py:26
  608.3 2.8 gather_fusion
  611.1 0.3 copy.11
  611.4 0.0 copy-done
  611.4 0.3 convolution_bitcast_fusion
  611.8 16.2 all-reduce.4
  627.9 0.1 copy.12
  628.1 2.3 fusion.2
  630.3 1.1 convolution_convert_fusion
  631.4 0.3 convolution_select_fusion
  631.7 0.3 copy.14
  632.1 4.3 broadcast_in_dim.34
  636.3 3.3 scatter_fusion
  639.7 9.3 all-to-all-start
  649.0 0.0 all-reduce.3.cloned.1.call-start
  649.1 0.9 fusion.18
  649.9 0.0 all-reduce.3.cloned.1.call-update
  650.0 1.6 fusion.15
  651.6 370.1 %all-to-all-done = f32[128,128,128]{2,1,0:T(8,128)} async-done(((f32[128,128,128]{2,1,0:T(8,128)}), f32[128,128,128]{2,1,0:T(8,128)}, u32[]{:S(2)}, u32[]{:S(2)}) %all-to-all-start) | async-done | bytes 8388640 | tf_op jit(solution)/shard_map/all_to_all | solution.py:43
  1021.7 4.4 reduce_sum.9
  1026.1 723.2 %all-reduce.3.cloned.1.call-done = f32[128,256]{1,0:T(8,128)} async-done(((f32[128,256]{1,0:T(8,128)}), f32[128,256]{1,0:T(8,128)}) %all-reduce.3.cloned.1.call-update) | async-done | bytes 131088 | tf_op jit(solution)/shard_map/psum | solution.py:38
  1749.3 1.6 copy.23
  (2 shorter events, 0.0 us)
Async XLA Ops:
  7.2 604.2 %copy-start = (bf16[4,1,4,128,128]{4,3,2,1,0:T(8,128)(2,1)S(1)}, bf16[4,1,4,128,128]{4,3,2,1,0:T(8,128)(2,1)}, u32[]{:S(2)}) copy-start(bf16[4,1,4,128,128]{4,3,2,1,0:T(8,128)(2,1)} %param.11) | copy-start | bytes 1572868
  7.2 601.1 %all-gather.2.cloned.1.call-start = ((), (), s32[]{:S(2)}) async-start(), calls=%async_computation.1 | async-start | bytes 4227072 | tf_op jit(solution)/shard_map/all_gather | solution.py:26
  639.7 382.0 %all-to-all-start = ((f32[128,128,128]{2,1,0:T(8,128)}), f32[128,128,128]{2,1,0:T(8,128)}, u32[]{:S(2)}, u32[]{:S(2)}) async-start(f32[128,128,128]{2,1,0:T(8,128)} %scatter_fusion), calls=%async_computation | async-start | bytes 16777216 | tf_op jit(solution)/shard_map/all_to_all | solution.py:43
  649.0 1100.2 %all-reduce.3.cloned.1.call-start = ((), (), s32[]{:S(2)}) async-start(), calls=%async_computation.2 | async-start | bytes 262144 | tf_op jit(solution)/shard_map/psum | solution.py:38
Sparse Core Ops, SparseCore 0:
  10.1 598.1 all-gather.1
  653.3 1095.8 all-reduce.2
where the time goes:
time: 1760 us
  waiting for transfers between devices  1680 us (95%)
  blocking collectives  23.6 us (1%)
    psum x1, waiting for transfers between devices, body(): lax.psum(jnp.dot(aggregated.T, slope, preferred_element_type=jnp.float32)...  723 us
    all_gather x1, waiting for transfers between devices, body(): gathered = lax.all_gather(features, 'row', axis=0, tiled=True)  589 us
    all_to_all x1, waiting for transfers between devices, body(): lax.all_to_all(term, 'row', split_axis=0, concat_axis=0, tiled=True)  370 us
  transfers between devices with their start and end apart: 3, of which 3 were waited for; matrix products, arithmetic and copies ran while one was open for 1% of the time, Pallas kernels for 0%

commit v1 on v0

v1 whole, which is shorter than its diff:
```python
import jax
import jax.numpy as jnp
from jax import lax
from jax.sharding import Mesh, PartitionSpec as P

ROW = ("y", "z", "xl")
REP = ("xh", "c")
PLANE = ("y", "xl")
NY, NZ, NX = 4, 16, 2
NP = NY * NX
TILE = 128
CUT = TILE // NP


def exchange(array, axes):
    return lax.all_to_all(array, axes, split_axis=0, concat_axis=0, tiled=True)


def body(features, weight, upstream, tile_owners, tile_counts, tile_values):
    f32, bf16 = jnp.float32, jnp.bfloat16
    width = features.shape[1]
    owners = tile_owners[:, 0, :]
    counts = tile_counts[:, 0]
    values = tile_values[:, 0]
    blocks, slots = owners.shape
    total = blocks * slots
    active = jnp.arange(slots, dtype=jnp.int32)[None, :] < counts[:, None]
    code = jnp.where(active, owners, -1).reshape(total).astype(bf16)
    code_rows = jnp.broadcast_to(jnp.pad(code, (0, width - total))[None, None, :], (NP, CUT, width))

    first = exchange(jnp.concatenate([features.reshape(NP, CUT, width), code_rows], axis=1), PLANE)
    codes = first[:, CUT, :total].astype(jnp.int32).reshape(NP * total)
    table = exchange(jnp.broadcast_to(first[None, :, :CUT], (NZ, NP, CUT, width)), "z")
    place = jnp.arange(NZ * NP, dtype=jnp.int32)
    ident = ((place // NX) % NY) * (NZ * NX) + (place // NP) * NX + place % NX
    pick = (codes[:, None] == ident[None, :]).astype(bf16)
    wanted = jnp.dot(pick, table.reshape(NZ * NP, CUT * width), preferred_element_type=f32).astype(bf16)
    third = exchange(wanted.reshape(NP, total, CUT, width), PLANE)
    picked = third.transpose(1, 0, 2, 3).reshape(blocks, slots, TILE, width)
    partial_value = jnp.einsum("btij,btjf->bif", values, picked, preferred_element_type=f32).astype(bf16)

    halves = jnp.stack([upstream[:, :width], upstream[:, width:]])
    shared = lax.all_gather(jnp.concatenate([partial_value, halves]), REP, axis=0)
    aggregated = jnp.sum(shared[:, :blocks].astype(f32), axis=0).astype(bf16).reshape(blocks * TILE, width)
    upstream_all = jnp.concatenate([shared[:, blocks], shared[:, blocks + 1]], axis=-1).reshape(blocks * TILE, 2 * width)

    pre_act = jnp.dot(aggregated, weight, preferred_element_type=f32)
    hidden_all, pullback = jax.vjp(jax.nn.gelu, pre_act)
    hidden = lax.dynamic_slice_in_dim(hidden_all.astype(bf16), lax.axis_index(REP) * TILE, TILE, 0)
    slope = pullback(upstream_all.astype(f32))[0].astype(bf16)
    weight_part = jnp.dot(aggregated.T, slope, preferred_element_type=f32)
    back_rows = jnp.dot(slope, weight.T, preferred_element_type=f32).astype(bf16).reshape(blocks, TILE, width)
    parts = jnp.einsum("btji,bjf->btif", values, back_rows, preferred_element_type=f32).astype(bf16)

    parts = parts.reshape(total, NP, CUT, width).transpose(1, 0, 2, 3)
    weight_cut = weight_part.astype(bf16).reshape(NP, CUT, 2, width).transpose(0, 2, 1, 3)
    fifth = exchange(jnp.concatenate([parts, weight_cut], axis=1), PLANE)
    summed = jnp.dot(pick.T, fifth[:, :total].reshape(NP * total, CUT * width), preferred_element_type=f32).astype(bf16)
    weight_sum = jnp.sum(fifth[:, total:].astype(f32), axis=0).astype(bf16)
    sixth = exchange(
        jnp.concatenate(
            [summed.reshape(NZ, NP, CUT, width), jnp.broadcast_to(weight_sum[None], (NZ, 2, CUT, width))], axis=1
        ),
        "z",
    )
    sums = jnp.sum(sixth.astype(f32), axis=0).astype(bf16)
    last = exchange(
        jnp.concatenate([sums[:NP, None], jnp.broadcast_to(sums[None, NP:], (NP, 2, CUT, width))], axis=1), PLANE
    ).astype(f32)
    grad_features = last[:, 0].reshape(TILE, width)
    grad_weight = last[:, 1:].transpose(0, 2, 1, 3).reshape(TILE, 2 * width)
    return (hidden, grad_weight, grad_features)


def solution(mesh):
    parted = Mesh(mesh.devices.reshape(NY, NZ, NX, 2, 2), ROW + REP)
    in_specs = (
        P(ROW + REP, None),
        P(),
        P(ROW + REP, None),
        P(ROW, REP, None),
        P(ROW, REP),
        P(ROW, REP, None, None, None),
    )
    out_specs = (P(ROW + REP, None), P(), P(ROW + REP, None))
    return jax.shard_map(body, mesh=parted, in_specs=in_specs, out_specs=out_specs, check_vma=False)
```

time: 1760 us -> 155 us (0.09)
  the two profiles are of different devices: /device:TPU:2 before, /device:TPU:32 now
where the time goes in v1:
time: 155 us; the launch traced here: 154 us
  waiting for transfers between devices  74.4 us (48%)
  blocking collectives  35.5 us (23%)
  starting transfers between devices  30 us (19%)
  local copies, waits for them, and re-layouts  6.96 us (4%)
  other arithmetic  4.04 us (3%)
  matrix products  2.34 us (2%)
    all_to_all x4, waiting for transfers between devices, exchange(): return lax.all_to_all(array, axes, split_axis=0, concat_axis=0, tiled=True)  74.4 us
    all_to_all x4, starting transfers between devices, exchange(): return lax.all_to_all(array, axes, split_axis=0, concat_axis=0, tiled=True)  30 us
    all_to_all x2, blocking collectives, exchange(): return lax.all_to_all(array, axes, split_axis=0, concat_axis=0, tiled=True)  25.6 us
    all_gather x1, blocking collectives, body(): lax.all_gather(jnp.concatenate([partial_value, halves]), REP, axis=0)  9.83 us
    unnamed x18, local copies, waits for them, and re-layouts  3.61 us
  transfers between devices with their start and end apart: 4, of which 4 were waited for; matrix products, arithmetic and copies ran while one was open for 1% of the time, Pallas kernels for 0%

profile of v1, /device:TPU:32, one launch (start us, length us, event | category | flops | bytes accessed | tf_op | source)
XLA Modules:
  0.0 154.2 jit_solution(16496179225823208258)
XLA Ops:
  0.7 0.7 copy-done.5
  1.5 0.5 broadcast.154
  2.0 1.3 reduce.10
  3.5 11.5 %all_to_all.30 = bf16[8,32,128]{2,1,0:T(8,128)(2,1)S(1)} all-to-all(bf16[8,32,128]{2,1,0:T(8,128)(2,1)S(1)} %pad_maximum_fusion.4), channel_id=1, replica_groups=mesh['y'=4,'z'=16,'xl'=2,'xh'=2,'c'=2] {'y','xl'}, dimensions={0} | all-to-all | bytes 131072 | tf_op jit(solution)/shard_map/all_to_all | solution.py:16
  15.0 0.9 broadcast_in_dim.16
  15.9 15.2 %all-to-all-start.1 = ((bf16[16,8,16,128]{3,2,1,0:T(8,128)(2,1)}), bf16[16,8,16,128]{3,2,1,0:T(8,128)(2,1)S(1)}, u32[]{:S(2)}, u32[]{:S(2)}) async-start(bf16[16,8,16,128]{3,2,1,0:T(8,128)(2,1)} %broadcast_in_dim.16), calls=%async_computation.1 | async-start | bytes 1048576 | tf_op jit(solution)/shard_map/all_to_all | solution.py:16
  31.3 27.1 %all-to-all-done.1 = bf16[16,8,16,128]{3,2,1,0:T(8,128)(2,1)S(1)} async-done(((bf16[16,8,16,128]{3,2,1,0:T(8,128)(2,1)}), bf16[16,8,16,128]{3,2,1,0:T(8,128)(2,1)S(1)}, u32[]{:S(2)}, u32[]{:S(2)}) %all-to-all-start.1) | async-done | bytes 524320 | tf_op jit(solution)/shard_map/all_to_all | solution.py:16
  58.4 0.3 fusion
  58.7 0.9 copy.75
  59.6 3.6 %all-to-all-start.2 = ((bf16[8,16,16,128]{3,2,1,0:T(8,128)(2,1)}), bf16[8,16,16,128]{3,2,1,0:T(8,128)(2,1)S(1)}, u32[]{:S(2)}, u32[]{:S(2)}) async-start(bf16[8,16,16,128]{3,2,1,0:T(8,128)(2,1)} %bitcast.38), calls=%async_computation.2 | async-start | bytes 1048576 | tf_op jit(solution)/shard_map/all_to_all | solution.py:16
  63.5 0.3 copy.55
  63.8 8.1 %all-to-all-done.2 = bf16[8,16,16,128]{3,2,1,0:T(8,128)(2,1)S(1)} async-done(((bf16[8,16,16,128]{3,2,1,0:T(8,128)(2,1)}), bf16[8,16,16,128]{3,2,1,0:T(8,128)(2,1)S(1)}, u32[]{:S(2)}, u32[]{:S(2)}) %all-to-all-start.2) | async-done | bytes 524320 | tf_op jit(solution)/shard_map/all_to_all | solution.py:16
  71.9 0.3 fusion.3
  72.3 0.2 copy.50
  72.5 9.8 %all-gather = bf16[24,128,128]{2,1,0:T(8,128)(2,1)S(1)} all-gather(bf16[6,128,128]{2,1,0:T(8,128)(2,1)S(1)} %copy.50), channel_id=2, replica_groups=mesh['y'=4,'z'=16,'xl'=2,'xh'=2,'c'=2] {'xh','c'}, dimensions={0}, use_global_device_ids=true | all-gather | bytes 983040 | tf_op jit(solution)/shard_map/all_gather | solution.py:43
  82.4 0.5 fusion.6
  83.0 0.2 convolution_convert_fusion.3
  83.2 0.2 convolution_convert_fusion.2
  83.5 0.3 fusion.34
  83.9 14.1 %all_to_all.31 = bf16[8,18,16,128]{3,2,1,0:T(8,128)(2,1)S(1)} all-to-all(bf16[8,18,16,128]{3,2,1,0:T(8,128)(2,1)S(1)} %pad_maximum_fusion.1), channel_id=1, replica_groups=mesh['y'=4,'z'=16,'xl'=2,'xh'=2,'c'=2] {'y','xl'}, dimensions={0} | all-to-all | bytes 1179648 | tf_op jit(solution)/shard_map/all_to_all | solution.py:16
  98.1 0.4 fusion.1
  98.6 0.9 pad_maximum_fusion
  99.6 7.8 %all-to-all-start.4 = ((bf16[16,10,16,128]{3,2,1,0:T(8,128)(2,1)}), bf16[16,10,16,128]{3,2,1,0:T(8,128)(2,1)S(1)}, u32[]{:S(2)}, u32[]{:S(2)}) async-start(bf16[16,10,16,128]{3,2,1,0:T(8,128)(2,1)} %pad_maximum_fusion), calls=%async_computation.4 | async-start | bytes 1310720 | tf_op jit(solution)/shard_map/all_to_all | solution.py:16
  107.4 33.4 %all-to-all-done.4 = bf16[16,10,16,128]{3,2,1,0:T(8,128)(2,1)S(1)} async-done(((bf16[16,10,16,128]{3,2,1,0:T(8,128)(2,1)}), bf16[16,10,16,128]{3,2,1,0:T(8,128)(2,1)S(1)}, u32[]{:S(2)}, u32[]{:S(2)}) %all-to-all-start.4) | async-done | bytes 655392 | tf_op jit(solution)/shard_map/all_to_all | solution.py:16
  140.9 0.6 copy-done.2
  141.6 0.7 slice-done
  142.2 0.7 pad_maximum_fusion.3
  142.9 3.4 %all-to-all-start.5 = ((bf16[8,3,16,128]{3,2,1,0:T(8,128)(2,1)}), bf16[8,3,16,128]{3,2,1,0:T(8,128)(2,1)S(1)}, u32[]{:S(2)}, u32[]{:S(2)}) async-start(bf16[8,3,16,128]{3,2,1,0:T(8,128)(2,1)} %pad_maximum_fusion.3), calls=%async_computation.5 | async-start | bytes 196608 | tf_op jit(solution)/shard_map/all_to_all | solution.py:16
  146.3 0.7 fusion.18
  146.9 5.8 %all-to-all-done.5 = bf16[8,3,16,128]{3,2,1,0:T(8,128)(2,1)S(1)} async-done(((bf16[8,3,16,128]{3,2,1,0:T(8,128)(2,1)}), bf16[8,3,16,128]{3,2,1,0:T(8,128)(2,1)S(1)}, u32[]{:S(2)}, u32[]{:S(2)}) %all-to-all-start.5) | async-done | bytes 98336 | tf_op jit(solution)/shard_map/all_to_all | solution.py:16
  152.9 0.7 copy.91
  153.5 0.6 slice.62
  (46 shorter events, 1.4 us)
Async XLA Ops:
  0.6 81.8 %copy-start = (bf16[128,256]{1,0:T(8,128)(2,1)S(1)}, bf16[128,256]{1,0:T(8,128)(2,1)}, u32[]{:S(2)}) copy-start(bf16[128,256]{1,0:T(8,128)(2,1)} %param.7) | copy-start | bytes 196612
  0.6 0.7 copy-start.5
  0.7 2.8 %copy-start.4 = (bf16[128,128]{1,0:T(8,128)(2,1)S(1)}, bf16[128,128]{1,0:T(8,128)(2,1)}, u32[]{:S(2)}) copy-start(bf16[128,128]{1,0:T(8,128)(2,1)} %param.6) | copy-start | bytes 98308
  15.9 42.4 %all-to-all-start.1 = ((bf16[16,8,16,128]{3,2,1,0:T(8,128)(2,1)}), bf16[16,8,16,128]{3,2,1,0:T(8,128)(2,1)S(1)}, u32[]{:S(2)}, u32[]{:S(2)}) async-start(bf16[16,8,16,128]{3,2,1,0:T(8,128)(2,1)} %broadcast_in_dim.16), calls=%async_computation.1 | async-start | bytes 1048576 | tf_op jit(solution)/shard_map/all_to_all | solution.py:16
  59.6 3.6 %copy-start.3 = (bf16[128,256]{1,0:T(8,128)(2,1)S(1)}, bf16[128,256]{1,0:T(8,128)(2,1)}, u32[]{:S(2)}) copy-start(bf16[128,256]{1,0:T(8,128)(2,1)} %param.8) | copy-start | bytes 196612
  59.6 3.9 %copy-start.1 = (bf16[4,1,4,128,128]{4,3,2,1,0:T(8,128)(2,1)S(1)}, bf16[4,1,4,128,128]{4,3,2,1,0:T(8,128)(2,1)}, u32[]{:S(2)}) copy-start(bf16[4,1,4,128,128]{4,3,2,1,0:T(8,128)(2,1)} %param.11) | copy-start | bytes 1572868
  59.6 12.3 %all-to-all-start.2 = ((bf16[8,16,16,128]{3,2,1,0:T(8,128)(2,1)}), bf16[8,16,16,128]{3,2,1,0:T(8,128)(2,1)S(1)}, u32[]{:S(2)}, u32[]{:S(2)}) async-start(bf16[8,16,16,128]{3,2,1,0:T(8,128)(2,1)} %bitcast.38), calls=%async_computation.2 | async-start | bytes 1048576 | tf_op jit(solution)/shard_map/all_to_all | solution.py:16
  99.6 41.2 %all-to-all-start.4 = ((bf16[16,10,16,128]{3,2,1,0:T(8,128)(2,1)}), bf16[16,10,16,128]{3,2,1,0:T(8,128)(2,1)S(1)}, u32[]{:S(2)}, u32[]{:S(2)}) async-start(bf16[16,10,16,128]{3,2,1,0:T(8,128)(2,1)} %pad_maximum_fusion), calls=%async_computation.4 | async-start | bytes 1310720 | tf_op jit(solution)/shard_map/all_to_all | solution.py:16
  140.9 0.6 copy-start.2
  141.5 0.7 slice-start
  142.9 9.8 %all-to-all-start.5 = ((bf16[8,3,16,128]{3,2,1,0:T(8,128)(2,1)}), bf16[8,3,16,128]{3,2,1,0:T(8,128)(2,1)S(1)}, u32[]{:S(2)}, u32[]{:S(2)}) async-start(bf16[8,3,16,128]{3,2,1,0:T(8,128)(2,1)} %pad_maximum_fusion.3), calls=%async_computation.5 | async-start | bytes 196608 | tf_op jit(solution)/shard_map/all_to_all | solution.py:16

commit v2 on v1

v2 whole, which is shorter than its diff:
```python
import jax
import jax.numpy as jnp
from jax import lax
from jax.sharding import Mesh, PartitionSpec as P

ROW = ("y", "zq", "zp", "xl")
REP = ("xh", "c")
NEAR = ("y", "zp", "xl")
NY, NQ, NZP, NX = 4, 8, 2, 2
NM = NY * NZP * NX
TILE = 128
CUT = TILE // NM


def exchange(array, axes):
    return lax.all_to_all(array, axes, split_axis=0, concat_axis=0, tiled=True)


def split(array):
    high = lax.reduce_precision(array, 8, 7)
    return jnp.concatenate([high.astype(jnp.bfloat16), (array - high).astype(jnp.bfloat16)])


def body(features, weight, upstream, tile_owners, tile_counts, tile_values):
    f32, bf16 = jnp.float32, jnp.bfloat16
    width = features.shape[1]
    owners = tile_owners[:, 0, :]
    counts = tile_counts[:, 0]
    values = tile_values[:, 0]
    blocks, slots = owners.shape
    total = blocks * slots
    active = jnp.arange(slots, dtype=jnp.int32)[None, :] < counts[:, None]
    code = jnp.where(active, owners, -1).reshape(total).astype(bf16)
    code_rows = jnp.broadcast_to(jnp.pad(code, (0, width - total))[None, None, :], (NM, CUT, width))

    first = exchange(jnp.concatenate([features.reshape(NM, CUT, width), code_rows], axis=1), NEAR)
    codes = first[:, CUT, :total].astype(jnp.int32).reshape(NM * total)
    table = exchange(jnp.broadcast_to(first[None, :, :CUT], (NQ, NM, CUT, width)), "zq")
    place = jnp.arange(NQ * NM, dtype=jnp.int32)
    ident = ((place // (NZP * NX)) % NY) * (NQ * NZP * NX) + (place // NM) * (NZP * NX) + place % (NZP * NX)
    pick = (codes[:, None] == ident[None, :]).astype(bf16)
    wanted = jnp.dot(pick, table.reshape(NQ * NM, CUT * width), preferred_element_type=f32).astype(bf16)
    third = exchange(wanted.reshape(NM, total, CUT, width), NEAR)
    picked = third.transpose(1, 0, 2, 3).reshape(blocks, slots, TILE, width)
    partial_value = jnp.einsum("btij,btjf->bif", values, picked, preferred_element_type=f32)

    pair = lax.all_gather(split(partial_value), "c", axis=0).reshape(2, 2, 2, 2, TILE, width)
    own_half = lax.dynamic_index_in_dim(pair, lax.axis_index("c"), 3, keepdims=False)
    half_sum = jnp.sum(own_half.astype(f32), axis=(0, 1))
    halves = jnp.stack([upstream[:, :width], upstream[:, width:]])
    far = lax.all_gather(jnp.concatenate([split(half_sum), halves]), "xh", axis=0)
    half_total = jnp.sum(far[:, :4].reshape(2, 2, 2, TILE, width).astype(f32), axis=(0, 1)).astype(bf16)
    shared = lax.all_gather(jnp.concatenate([half_total, far[0, 4:], far[1, 4:]]), "c", axis=0)
    aggregated = shared[:, :2].transpose(1, 0, 2, 3).reshape(blocks * TILE, width)
    upstream_all = shared[:, 2:].reshape(2, 2, 2, TILE, width).transpose(1, 0, 3, 2, 4).reshape(blocks * TILE, 2 * width)

    pre_act = jnp.dot(aggregated, weight, preferred_element_type=f32)
    hidden_all, pullback = jax.vjp(jax.nn.gelu, pre_act)
    hidden = lax.dynamic_slice_in_dim(hidden_all.astype(bf16), lax.axis_index(REP) * TILE, TILE, 0)
    slope = pullback(upstream_all.astype(f32))[0].astype(bf16)
    weight_part = jnp.dot(aggregated.T, slope, preferred_element_type=f32)
    back_rows = jnp.dot(slope, weight.T, preferred_element_type=f32).astype(bf16).reshape(blocks, TILE, width)
    parts = jnp.einsum("btji,bjf->btif", values, back_rows, preferred_element_type=f32).astype(bf16)

    parts = parts.reshape(total, NM, CUT, width).transpose(1, 0, 2, 3)
    weight_cut = weight_part.astype(bf16).reshape(NM, CUT, 2, width).transpose(0, 2, 1, 3)
    fifth = exchange(jnp.concatenate([parts, weight_cut], axis=1), NEAR)
    summed = jnp.dot(pick.T, fifth[:, :total].reshape(NM * total, CUT * width), preferred_element_type=f32).astype(bf16)
    weight_sum = jnp.sum(fifth[:, total:].astype(f32), axis=0).astype(bf16)
    sixth = exchange(
        jnp.concatenate(
            [summed.reshape(NQ, NM, CUT, width), jnp.broadcast_to(weight_sum[None], (NQ, 2, CUT, width))], axis=1
        ),
        "zq",
    )
    sums = jnp.sum(sixth.astype(f32), axis=0).astype(bf16)
    last = exchange(
        jnp.concatenate([sums[:NM, None], jnp.broadcast_to(sums[None, NM:], (NM, 2, CUT, width))], axis=1), NEAR
    ).astype(f32)
    grad_features = last[:, 0].reshape(TILE, width)
    grad_weight = last[:, 1:].transpose(0, 2, 1, 3).reshape(TILE, 2 * width)
    return (hidden, grad_weight, grad_features)


def solution(mesh):
    parted = Mesh(mesh.devices.reshape(NY, NQ, NZP, NX, 2, 2), ROW + REP)
    in_specs = (
        P(ROW + REP, None),
        P(),
        P(ROW + REP, None),
        P(ROW, REP, None),
        P(ROW, REP),
        P(ROW, REP, None, None, None),
    )
    out_specs = (P(ROW + REP, None), P(), P(ROW + REP, None))
    return jax.shard_map(body, mesh=parted, in_specs=in_specs, out_specs=out_specs, check_vma=False)
```

time: 155 us -> 137 us (0.88)
  the two profiles are of different devices: /device:TPU:32 before, /device:TPU:4 now
where the time goes in v2:
time: 137 us
  blocking collectives  67.6 us (49%)
  waiting for transfers between devices  34.8 us (25%)
  starting transfers between devices  21.5 us (16%)
  local copies, waits for them, and re-layouts  6.28 us (5%)
  other arithmetic  3.28 us (2%)
  matrix products  2.24 us (2%)
    all_to_all x3, blocking collectives, exchange(): return lax.all_to_all(array, axes, split_axis=0, concat_axis=0, tiled=True)  54.3 us
    all_to_all x3, waiting for transfers between devices, exchange(): return lax.all_to_all(array, axes, split_axis=0, concat_axis=0, tiled=True)  34.8 us
    all_to_all x3, starting transfers between devices, exchange(): return lax.all_to_all(array, axes, split_axis=0, concat_axis=0, tiled=True)  21.5 us
    all_gather x1, blocking collectives, body(): lax.all_gather(jnp.concatenate([split(half_sum), halves]), 'xh', axis=0)  9.12 us
  transfers between devices with their start and end apart: 3, of which 3 were waited for; matrix products, arithmetic and copies ran while one was open for 1% of the time, Pallas kernels for 0%

profile of v2, /device:TPU:4, one launch (start us, length us, event | category | flops | bytes accessed | tf_op | source)
XLA Modules:
  0.0 136.7 jit_solution(3751594114248153766)
XLA Ops:
  0.7 0.7 copy-done.4
  1.5 0.5 broadcast.154
  2.0 1.3 reduce.13
  3.5 13.6 %all_to_all.30 = bf16[16,16,128]{2,1,0:T(8,128)(2,1)S(1)} all-to-all(bf16[16,16,128]{2,1,0:T(8,128)(2,1)S(1)} %pad_maximum_fusion.6), channel_id=1, replica_groups=mesh['y'=4,'zq'=8,'zp'=2,'xl'=2,'xh'=2,'c'=2] {'y','zp','xl'}, dimensions={0} | all-to-all | bytes 131072 | tf_op jit(solution)/shard_map/all_to_all | solution.py:16
  17.1 0.7 broadcast_in_dim.16
  17.8 14.2 %all-to-all-start.1 = ((bf16[8,16,8,128]{3,2,1,0:T(8,128)(2,1)}), bf16[8,16,8,128]{3,2,1,0:T(8,128)(2,1)S(1)}, u32[]{:S(2)}, u32[]{:S(2)}) async-start(bf16[8,16,8,128]{3,2,1,0:T(8,128)(2,1)} %broadcast_in_dim.16), calls=%async_computation.1 | async-start | bytes 524288 | tf_op jit(solution)/shard_map/all_to_all | solution.py:16
  32.1 19.8 %all-to-all-done.1 = bf16[8,16,8,128]{3,2,1,0:T(8,128)(2,1)S(1)} async-done(((bf16[8,16,8,128]{3,2,1,0:T(8,128)(2,1)}), bf16[8,16,8,128]{3,2,1,0:T(8,128)(2,1)S(1)}, u32[]{:S(2)}, u32[]{:S(2)}) %all-to-all-start.1) | async-done | bytes 262176 | tf_op jit(solution)/shard_map/all_to_all | solution.py:16
  51.9 0.3 fusion
  52.2 0.9 copy.55
  53.1 3.7 %all-to-all-start.2 = ((bf16[16,16,8,128]{3,2,1,0:T(8,128)(2,1)}), bf16[16,16,8,128]{3,2,1,0:T(8,128)(2,1)S(1)}, u32[]{:S(2)}, u32[]{:S(2)}) async-start(bf16[16,16,8,128]{3,2,1,0:T(8,128)(2,1)} %bitcast.45), calls=%async_computation.2 | async-start | bytes 1048576 | tf_op jit(solution)/shard_map/all_to_all | solution.py:16
  57.1 0.3 copy.47
  57.4 8.3 %all-to-all-done.2 = bf16[16,16,8,128]{3,2,1,0:T(8,128)(2,1)S(1)} async-done(((bf16[16,16,8,128]{3,2,1,0:T(8,128)(2,1)}), bf16[16,16,8,128]{3,2,1,0:T(8,128)(2,1)S(1)}, u32[]{:S(2)}, u32[]{:S(2)}) %all-to-all-start.2) | async-done | bytes 524320 | tf_op jit(solution)/shard_map/all_to_all | solution.py:16
  65.9 0.3 reduce-precision_convert_fusion
  66.3 0.2 copy.40
  66.4 2.2 %all-gather = bf16[16,128,128]{2,1,0:T(8,128)(2,1)S(1)} all-gather(bf16[8,128,128]{2,1,0:T(8,128)(2,1)S(1)} %copy.40), channel_id=2, replica_groups=mesh['y'=4,'zq'=8,'zp'=2,'xl'=2,'xh'=2,'c'=2] {'c'}, dimensions={0}, use_global_device_ids=true | all-gather | bytes 786432 | tf_op jit(solution)/shard_map/all_gather | solution.py:47
  68.6 0.2 copy.51
  69.1 9.1 %all-gather.1 = bf16[12,128,128]{2,1,0:T(8,128)(2,1)S(1)} all-gather(bf16[6,128,128]{2,1,0:T(8,128)(2,1)S(1)} %copy.44), channel_id=3, replica_groups=mesh['y'=4,'zq'=8,'zp'=2,'xl'=2,'xh'=2,'c'=2] {'xh'}, dimensions={0}, use_global_device_ids=true | all-gather | bytes 589824 | tf_op jit(solution)/shard_map/all_gather | solution.py:51
  78.4 2.1 %all-gather.2 = bf16[12,128,128]{2,1,0:T(8,128)(2,1)S(1)} all-gather(bf16[6,128,128]{2,1,0:T(8,128)(2,1)S(1)} %pad_maximum_fusion.4), channel_id=4, replica_groups=mesh['y'=4,'zq'=8,'zp'=2,'xl'=2,'xh'=2,'c'=2] {'c'}, dimensions={0}, use_global_device_ids=true | all-gather | bytes 589824 | tf_op jit(solution)/shard_map/all_gather | solution.py:53
  80.5 0.4 copy.46
  81.0 0.5 fusion.9
  81.5 0.2 fusion.2
  81.7 0.2 convolution_convert_fusion.2
  81.9 0.3 fusion.34
  82.5 15.3 %all_to_all.31 = bf16[16,18,8,128]{3,2,1,0:T(8,128)(2,1)S(1)} all-to-all(bf16[16,18,8,128]{3,2,1,0:T(8,128)(2,1)S(1)} %pad_maximum_fusion), channel_id=1, replica_groups=mesh['y'=4,'zq'=8,'zp'=2,'xl'=2,'xh'=2,'c'=2] {'y','zp','xl'}, dimensions={0} | all-to-all | bytes 1179648 | tf_op jit(solution)/shard_map/all_to_all | solution.py:16
  97.8 0.3 fusion.1
  98.3 25.4 %all_to_all.32 = bf16[8,18,8,128]{3,2,1,0:T(8,128)(2,1)S(1)} all-to-all(bf16[8,18,8,128]{3,2,1,0:T(8,128)(2,1)S(1)} %pad_maximum_fusion.1), channel_id=1, replica_groups=mesh['y'=4,'zq'=8,'zp'=2,'xl'=2,'xh'=2,'c'=2] {'zq'}, dimensions={0} | all-to-all | bytes 589824 | tf_op jit(solution)/shard_map/all_to_all | solution.py:16
  123.8 0.7 pad_maximum_fusion.5
  124.5 3.6 %all-to-all-start.5 = ((bf16[16,3,8,128]{3,2,1,0:T(8,128)(2,1)}), bf16[16,3,8,128]{3,2,1,0:T(8,128)(2,1)S(1)}, u32[]{:S(2)}, u32[]{:S(2)}) async-start(bf16[16,3,8,128]{3,2,1,0:T(8,128)(2,1)} %pad_maximum_fusion.5), calls=%async_computation.5 | async-start | bytes 196608 | tf_op jit(solution)/shard_map/all_to_all | solution.py:16
  128.1 0.7 fusion.21
  128.7 6.6 %all-to-all-done.5 = bf16[16,3,8,128]{3,2,1,0:T(8,128)(2,1)S(1)} async-done(((bf16[16,3,8,128]{3,2,1,0:T(8,128)(2,1)}), bf16[16,3,8,128]{3,2,1,0:T(8,128)(2,1)S(1)}, u32[]{:S(2)}, u32[]{:S(2)}) %all-to-all-start.5) | async-done | bytes 98336 | tf_op jit(solution)/shard_map/all_to_all | solution.py:16
  135.4 0.7 slice_bitcast_fusion
  136.1 0.6 slice_bitcast_fusion.2
  (51 shorter events, 1.8 us)
Async XLA Ops:
  0.6 80.3 %copy-start = (bf16[128,256]{1,0:T(8,128)(2,1)S(1)}, bf16[128,256]{1,0:T(8,128)(2,1)}, u32[]{:S(2)}) copy-start(bf16[128,256]{1,0:T(8,128)(2,1)} %param.7) | copy-start | bytes 196612
  0.6 0.7 copy-start.4
  0.7 2.8 %copy-start.3 = (bf16[128,128]{1,0:T(8,128)(2,1)S(1)}, bf16[128,128]{1,0:T(8,128)(2,1)}, u32[]{:S(2)}) copy-start(bf16[128,128]{1,0:T(8,128)(2,1)} %param.6) | copy-start | bytes 98308
  17.8 34.1 %all-to-all-start.1 = ((bf16[8,16,8,128]{3,2,1,0:T(8,128)(2,1)}), bf16[8,16,8,128]{3,2,1,0:T(8,128)(2,1)S(1)}, u32[]{:S(2)}, u32[]{:S(2)}) async-start(bf16[8,16,8,128]{3,2,1,0:T(8,128)(2,1)} %broadcast_in_dim.16), calls=%async_computation.1 | async-start | bytes 524288 | tf_op jit(solution)/shard_map/all_to_all | solution.py:16
  53.1 3.7 %copy-start.2 = (bf16[128,256]{1,0:T(8,128)(2,1)S(1)}, bf16[128,256]{1,0:T(8,128)(2,1)}, u32[]{:S(2)}) copy-start(bf16[128,256]{1,0:T(8,128)(2,1)} %param.8) | copy-start | bytes 196612
  53.1 4.0 %copy-start.1 = (bf16[4,1,4,128,128]{4,3,2,1,0:T(8,128)(2,1)S(1)}, bf16[4,1,4,128,128]{4,3,2,1,0:T(8,128)(2,1)}, u32[]{:S(2)}) copy-start(bf16[4,1,4,128,128]{4,3,2,1,0:T(8,128)(2,1)} %param.11) | copy-start | bytes 1572868
  53.1 12.6 %all-to-all-start.2 = ((bf16[16,16,8,128]{3,2,1,0:T(8,128)(2,1)}), bf16[16,16,8,128]{3,2,1,0:T(8,128)(2,1)S(1)}, u32[]{:S(2)}, u32[]{:S(2)}) async-start(bf16[16,16,8,128]{3,2,1,0:T(8,128)(2,1)} %bitcast.45), calls=%async_computation.2 | async-start | bytes 1048576 | tf_op jit(solution)/shard_map/all_to_all | solution.py:16
  124.5 10.9 %all-to-all-start.5 = ((bf16[16,3,8,128]{3,2,1,0:T(8,128)(2,1)}), bf16[16,3,8,128]{3,2,1,0:T(8,128)(2,1)S(1)}, u32[]{:S(2)}, u32[]{:S(2)}) async-start(bf16[16,3,8,128]{3,2,1,0:T(8,128)(2,1)} %pad_maximum_fusion.5), calls=%async_computation.5 | async-start | bytes 196608 | tf_op jit(solution)/shard_map/all_to_all | solution.py:16

commit v3 on v2

--- a/solution.py
+++ b/solution.py
@@ -13,7 +13,8 @@
 
 
 def exchange(array, axes):
-    return lax.all_to_all(array, axes, split_axis=0, concat_axis=0, tiled=True)
+    flat = array.reshape(array.shape[0], -1, array.shape[-1])
+    return lax.all_to_all(flat, axes, split_axis=0, concat_axis=0, tiled=True).reshape(array.shape)
 
 
 def split(array):
@@ -30,16 +31,22 @@
     blocks, slots = owners.shape
     total = blocks * slots
     active = jnp.arange(slots, dtype=jnp.int32)[None, :] < counts[:, None]
+    wide = exchange(jnp.broadcast_to(features[None], (NQ, TILE, width)), "zq")
     code = jnp.where(active, owners, -1).reshape(total).astype(bf16)
-    code_rows = jnp.broadcast_to(jnp.pad(code, (0, width - total))[None, None, :], (NM, CUT, width))
+    code_rows = jnp.broadcast_to(jnp.pad(code, (0, width - total))[None, None, None, :], (NM, 1, CUT, width))
+    halves = jnp.stack([upstream[:, :width], upstream[:, width:]])
+    upstream_all = lax.all_gather(lax.all_gather(halves, "xh", axis=0), "c", axis=1)
+    wide, code_rows, upstream_all = lax.optimization_barrier((wide, code_rows, upstream_all))
 
-    first = exchange(jnp.concatenate([features.reshape(NM, CUT, width), code_rows], axis=1), NEAR)
-    codes = first[:, CUT, :total].astype(jnp.int32).reshape(NM * total)
-    table = exchange(jnp.broadcast_to(first[None, :, :CUT], (NQ, NM, CUT, width)), "zq")
+    slices = wide.reshape(NQ, NM, CUT, width).transpose(1, 0, 2, 3)
+    second = exchange(jnp.concatenate([slices, code_rows], axis=1), NEAR)
+    codes = second[:, NQ, 0, :total].astype(jnp.int32).reshape(NM * total)
     place = jnp.arange(NQ * NM, dtype=jnp.int32)
-    ident = ((place // (NZP * NX)) % NY) * (NQ * NZP * NX) + (place // NM) * (NZP * NX) + place % (NZP * NX)
+    member = place // NQ
+    ident = (member // (NZP * NX)) * (NQ * NZP * NX) + (place % NQ) * (NZP * NX) + member % (NZP * NX)
     pick = (codes[:, None] == ident[None, :]).astype(bf16)
-    wanted = jnp.dot(pick, table.reshape(NQ * NM, CUT * width), preferred_element_type=f32).astype(bf16)
+    table = second[:, :NQ].reshape(NQ * NM, CUT * width)
+    wanted = jnp.dot(pick, table, preferred_element_type=f32).astype(bf16)
     third = exchange(wanted.reshape(NM, total, CUT, width), NEAR)
     picked = third.transpose(1, 0, 2, 3).reshape(blocks, slots, TILE, width)
     partial_value = jnp.einsum("btij,btjf->bif", values, picked, preferred_element_type=f32)
@@ -47,12 +54,10 @@
     pair = lax.all_gather(split(partial_value), "c", axis=0).reshape(2, 2, 2, 2, TILE, width)
     own_half = lax.dynamic_index_in_dim(pair, lax.axis_index("c"), 3, keepdims=False)
     half_sum = jnp.sum(own_half.astype(f32), axis=(0, 1))
-    halves = jnp.stack([upstream[:, :width], upstream[:, width:]])
-    far = lax.all_gather(jnp.concatenate([split(half_sum), halves]), "xh", axis=0)
-    half_total = jnp.sum(far[:, :4].reshape(2, 2, 2, TILE, width).astype(f32), axis=(0, 1)).astype(bf16)
-    shared = lax.all_gather(jnp.concatenate([half_total, far[0, 4:], far[1, 4:]]), "c", axis=0)
-    aggregated = shared[:, :2].transpose(1, 0, 2, 3).reshape(blocks * TILE, width)
-    upstream_all = shared[:, 2:].reshape(2, 2, 2, TILE, width).transpose(1, 0, 3, 2, 4).reshape(blocks * TILE, 2 * width)
+    far = lax.all_gather(split(half_sum), "xh", axis=0)
+    half_total = jnp.sum(far.reshape(2, 2, 2, TILE, width).astype(f32), axis=(0, 1)).astype(bf16)
+    aggregated = lax.all_gather(half_total, "c", axis=1).reshape(blocks * TILE, width)
+    upstream_all = upstream_all.transpose(0, 1, 3, 2, 4).reshape(blocks * TILE, 2 * width)
 
     pre_act = jnp.dot(aggregated, weight, preferred_element_type=f32)
     hidden_all, pullback = jax.vjp(jax.nn.gelu, pre_act)
@@ -69,7 +74,7 @@
     weight_sum = jnp.sum(fifth[:, total:].astype(f32), axis=0).astype(bf16)
     sixth = exchange(
         jnp.concatenate(
-            [summed.reshape(NQ, NM, CUT, width), jnp.broadcast_to(weight_sum[None], (NQ, 2, CUT, width))], axis=1
+            [summed.reshape(NM, NQ, CUT, width).transpose(1, 0, 2, 3), jnp.broadcast_to(weight_sum[None], (NQ, 2, CUT, width))], axis=1
         ),
         "zq",
     )

time: 137 us -> 137 us (level)
  blocking collectives: 67.6 us -> 61.1 us
  starting transfers between devices: 21.5 us -> 27.7 us
    all_to_all x3 -> x2, blocking collectives: 54.3 us -> 40.9 us  [exchange(): lax.all_to_all(flat, axes, split_axis=0, concat_axis=0, tiled=True)]
    all_gather x2 -> x4, blocking collectives: 11.2 us -> 18 us  [the longest x1 7.72 us: body(): far = lax.all_gather(split(half_sum), 'xh', axis=0)]
    all_to_all x3 -> x4, starting transfers between devices: 21.5 us -> 27.7 us  [exchange(): lax.all_to_all(flat, axes, split_axis=0, concat_axis=0, tiled=True)]
    reshape x0 -> x3, other arithmetic: none -> 1.47 us  [exchange(): flat = array.reshape(array.shape[0], -1, array.shape[-1])]
    all_to_all x3 -> x4, waiting for transfers between devices: 34.8 us -> 33.5 us  [exchange(): lax.all_to_all(flat, axes, split_axis=0, concat_axis=0, tiled=True)]
  transfers between devices with their start and end apart: 3 -> 4, of which waited for: 3 -> 4; matrix products, arithmetic and copies ran while one was open for 1% -> 2% of each run, Pallas kernels for 0% -> 0%
where the time goes in v3:
time: 137 us; the launch traced here: 136 us
  blocking collectives  61.1 us (45%)
  waiting for transfers between devices  33.5 us (24%)
  starting transfers between devices  27.7 us (20%)
  local copies, waits for them, and re-layouts  6.94 us (5%)
  other arithmetic  3.32 us (2%)
  matrix products  2.24 us (2%)
    all_to_all x2, blocking collectives, exchange(): lax.all_to_all(flat, axes, split_axis=0, concat_axis=0, tiled=True)  40.9 us
    all_to_all x4, waiting for transfers between devices, exchange(): lax.all_to_all(flat, axes, split_axis=0, concat_axis=0, tiled=True)  33.5 us
    all_to_all x4, starting transfers between devices, exchange(): lax.all_to_all(flat, axes, split_axis=0, concat_axis=0, tiled=True)  27.7 us
    all_gather x1, blocking collectives, body(): far = lax.all_gather(split(half_sum), 'xh', axis=0)  7.72 us
    all_gather x1, blocking collectives, body(): lax.all_gather(halves, 'xh', axis=0)  6.45 us
  transfers between devices with their start and end apart: 4, of which 4 were waited for; matrix products, arithmetic and copies ran while one was open for 2% of the time, Pallas kernels for 0%

profile of v3, /device:TPU:4, one launch (start us, length us, event | category | flops | bytes accessed | tf_op | source)
XLA Modules:
  0.0 135.8 jit_solution(13461103423770609252)
XLA Ops:
  0.6 1.5 %broadcast_in_dim.16 = bf16[8,128,128]{2,1,0:T(8,128)(2,1)} broadcast(bf16[128,128]{1,0:T(8,128)(2,1)} %param.6), dimensions={1,2} | broadcast | bytes 294912 | tf_op jit(solution)/shard_map/broadcast_in_dim | solution.py:34
  2.2 15.2 %all-to-all-start = ((bf16[8,128,128]{2,1,0:T(8,128)(2,1)}), bf16[8,128,128]{2,1,0:T(8,128)(2,1)S(1)}, u32[]{:S(2)}, u32[]{:S(2)}) async-start(bf16[8,128,128]{2,1,0:T(8,128)(2,1)} %broadcast_in_dim.16), calls=%async_computation | async-start | bytes 524288 | tf_op jit(solution)/shard_map/all_to_all | solution.py:17
  17.4 0.7 copy-done.4
  18.2 0.5 broadcast.158
  18.8 0.7 reduce.14
  19.6 6.4 %all-gather = bf16[4,128,128]{2,1,0:T(8,128)(2,1)S(1)} all-gather(bf16[2,128,128]{2,1,0:T(8,128)(2,1)S(1)} %pad_maximum_fusion.4), channel_id=2, replica_groups=mesh['y'=4,'zq'=8,'zp'=2,'xl'=2,'xh'=2,'c'=2] {'xh'}, dimensions={0}, use_global_device_ids=true | all-gather | bytes 196608 | tf_op jit(solution)/shard_map/all_gather | solution.py:38
  26.1 2.0 %all-gather.1 = bf16[2,4,128,128]{3,2,1,0:T(8,128)(2,1)S(1)} all-gather(bf16[2,2,128,128]{3,2,1,0:T(8,128)(2,1)S(1)} %bitcast.127), channel_id=3, replica_groups=mesh['y'=4,'zq'=8,'zp'=2,'xl'=2,'xh'=2,'c'=2] {'c'}, dimensions={1}, use_global_device_ids=true | all-gather | bytes 393216 | tf_op jit(solution)/shard_map/all_gather | solution.py:38
  28.0 10.7 %all-to-all-done = bf16[8,128,128]{2,1,0:T(8,128)(2,1)S(1)} async-done(((bf16[8,128,128]{2,1,0:T(8,128)(2,1)}), bf16[8,128,128]{2,1,0:T(8,128)(2,1)S(1)}, u32[]{:S(2)}, u32[]{:S(2)}) %all-to-all-start) | async-done | bytes 262176 | tf_op jit(solution)/shard_map/all_to_all | solution.py:17
  38.8 0.8 copy_bitcast_fusion.2
  39.5 5.2 %all-to-all-start.1 = ((bf16[16,72,128]{2,1,0:T(8,128)(2,1)}), bf16[16,72,128]{2,1,0:T(8,128)(2,1)S(1)}, u32[]{:S(2)}, u32[]{:S(2)}) async-start(bf16[16,72,128]{2,1,0:T(8,128)(2,1)} %copy_bitcast_fusion.2), calls=%async_computation.1 | async-start | bytes 589824 | tf_op jit(solution)/shard_map/all_to_all | solution.py:17
  44.8 8.0 %all-to-all-done.1 = bf16[16,72,128]{2,1,0:T(8,128)(2,1)S(1)} async-done(((bf16[16,72,128]{2,1,0:T(8,128)(2,1)}), bf16[16,72,128]{2,1,0:T(8,128)(2,1)S(1)}, u32[]{:S(2)}, u32[]{:S(2)}) %all-to-all-start.1) | async-done | bytes 294944 | tf_op jit(solution)/shard_map/all_to_all | solution.py:17
  52.9 0.3 convolution_convert_fusion
  53.3 1.0 reshape_reshape.3
  54.3 3.7 %all-to-all-start.2 = ((bf16[16,128,128]{2,1,0:T(8,128)(2,1)}), bf16[16,128,128]{2,1,0:T(8,128)(2,1)S(1)}, u32[]{:S(2)}, u32[]{:S(2)}) async-start(bf16[16,128,128]{2,1,0:T(8,128)(2,1)} %reshape_reshape.3), calls=%async_computation.2 | async-start | bytes 1048576 | tf_op jit(solution)/shard_map/all_to_all | solution.py:17
  58.0 0.3 copy.41
  58.3 0.4 copy.40
  58.8 8.1 %all-to-all-done.2 = bf16[16,128,128]{2,1,0:T(8,128)(2,1)S(1)} async-done(((bf16[16,128,128]{2,1,0:T(8,128)(2,1)}), bf16[16,128,128]{2,1,0:T(8,128)(2,1)S(1)}, u32[]{:S(2)}, u32[]{:S(2)}) %all-to-all-start.2) | async-done | bytes 524320 | tf_op jit(solution)/shard_map/all_to_all | solution.py:17
  67.0 0.4 reduce-precision_convert_fusion
  67.6 2.2 %all-gather.2 = bf16[16,128,128]{2,1,0:T(8,128)(2,1)S(1)} all-gather(bf16[8,128,128]{2,1,0:T(8,128)(2,1)S(1)} %copy.37), channel_id=4, replica_groups=mesh['y'=4,'zq'=8,'zp'=2,'xl'=2,'xh'=2,'c'=2] {'c'}, dimensions={0}, use_global_device_ids=true | all-gather | bytes 786432 | tf_op jit(solution)/shard_map/all_gather | solution.py:54
  70.2 7.7 %all-gather.3 = bf16[8,128,128]{2,1,0:T(8,128)(2,1)S(1)} all-gather(bf16[4,128,128]{2,1,0:T(8,128)(2,1)S(1)} %copy.39), channel_id=5, replica_groups=mesh['y'=4,'zq'=8,'zp'=2,'xl'=2,'xh'=2,'c'=2] {'xh'}, dimensions={0}, use_global_device_ids=true | all-gather | bytes 393216 | tf_op jit(solution)/shard_map/all_gather | solution.py:57
  78.0 1.9 %all-gather.4 = bf16[2,256,128]{2,1,0:T(8,128)(2,1)S(1)} all-gather(bf16[2,128,128]{2,1,0:T(8,128)(2,1)S(1)} %reduce_sum.55), channel_id=6, replica_groups=mesh['y'=4,'zq'=8,'zp'=2,'xl'=2,'xh'=2,'c'=2] {'c'}, dimensions={1}, use_global_device_ids=true | all-gather | bytes 196608 | tf_op jit(solution)/shard_map/all_gather | solution.py:59
  79.9 0.5 fusion.8
  80.9 0.3 fusion.30
  81.5 15.3 %all_to_all.30 = bf16[16,144,128]{2,1,0:T(8,128)(2,1)S(1)} all-to-all(bf16[16,144,128]{2,1,0:T(8,128)(2,1)S(1)} %maximum_bitcast_fusion), channel_id=1, replica_groups=mesh['y'=4,'zq'=8,'zp'=2,'xl'=2,'xh'=2,'c'=2] {'y','zp','xl'}, dimensions={0} | all-to-all | bytes 1179648 | tf_op jit(solution)/shard_map/all_to_all | solution.py:17
  96.8 0.3 fusion
  97.3 25.6 %all_to_all.31 = bf16[8,144,128]{2,1,0:T(8,128)(2,1)S(1)} all-to-all(bf16[8,144,128]{2,1,0:T(8,128)(2,1)S(1)} %bitcast.119), channel_id=1, replica_groups=mesh['y'=4,'zq'=8,'zp'=2,'xl'=2,'xh'=2,'c'=2] {'zq'}, dimensions={0} | all-to-all | bytes 589824 | tf_op jit(solution)/shard_map/all_to_all | solution.py:17
  122.9 0.7 maximum_bitcast_fusion.1
  123.6 3.6 %all-to-all-start.5 = ((bf16[16,24,128]{2,1,0:T(8,128)(2,1)}), bf16[16,24,128]{2,1,0:T(8,128)(2,1)S(1)}, u32[]{:S(2)}, u32[]{:S(2)}) async-start(bf16[16,24,128]{2,1,0:T(8,128)(2,1)} %maximum_bitcast_fusion.1), calls=%async_computation.5 | async-start | bytes 196608 | tf_op jit(solution)/shard_map/all_to_all | solution.py:17
  127.2 0.7 fusion.20
  127.8 6.6 %all-to-all-done.5 = bf16[16,24,128]{2,1,0:T(8,128)(2,1)S(1)} async-done(((bf16[16,24,128]{2,1,0:T(8,128)(2,1)}), bf16[16,24,128]{2,1,0:T(8,128)(2,1)S(1)}, u32[]{:S(2)}, u32[]{:S(2)}) %all-to-all-start.5) | async-done | bytes 98336 | tf_op jit(solution)/shard_map/all_to_all | solution.py:17
  134.5 0.7 slice_bitcast_fusion.1
  135.2 0.6 slice_bitcast_fusion.2
  (48 shorter events, 2.3 us)
Async XLA Ops:
  0.6 79.3 %copy-start = (bf16[128,256]{1,0:T(8,128)(2,1)S(1)}, bf16[128,256]{1,0:T(8,128)(2,1)}, u32[]{:S(2)}) copy-start(bf16[128,256]{1,0:T(8,128)(2,1)} %param.7) | copy-start | bytes 196612
  2.2 17.4 %copy-start.2 = (bf16[128,256]{1,0:T(8,128)(2,1)S(1)}, bf16[128,256]{1,0:T(8,128)(2,1)}, u32[]{:S(2)}) copy-start(bf16[128,256]{1,0:T(8,128)(2,1)} %param.8) | copy-start | bytes 196612
  2.2 36.6 %all-to-all-start = ((bf16[8,128,128]{2,1,0:T(8,128)(2,1)}), bf16[8,128,128]{2,1,0:T(8,128)(2,1)S(1)}, u32[]{:S(2)}, u32[]{:S(2)}) async-start(bf16[8,128,128]{2,1,0:T(8,128)(2,1)} %broadcast_in_dim.16), calls=%async_computation | async-start | bytes 524288 | tf_op jit(solution)/shard_map/all_to_all | solution.py:17
  17.4 0.7 copy-start.4
  18.1 0.7 copy-start.3
  39.5 13.3 %all-to-all-start.1 = ((bf16[16,72,128]{2,1,0:T(8,128)(2,1)}), bf16[16,72,128]{2,1,0:T(8,128)(2,1)S(1)}, u32[]{:S(2)}, u32[]{:S(2)}) async-start(bf16[16,72,128]{2,1,0:T(8,128)(2,1)} %copy_bitcast_fusion.2), calls=%async_computation.1 | async-start | bytes 589824 | tf_op jit(solution)/shard_map/all_to_all | solution.py:17
  54.3 3.7 %copy-start.1 = (bf16[4,1,4,128,128]{4,3,2,1,0:T(8,128)(2,1)S(1)}, bf16[4,1,4,128,128]{4,3,2,1,0:T(8,128)(2,1)}, u32[]{:S(2)}) copy-start(bf16[4,1,4,128,128]{4,3,2,1,0:T(8,128)(2,1)} %param.11) | copy-start | bytes 1572868
  54.3 12.6 %all-to-all-start.2 = ((bf16[16,128,128]{2,1,0:T(8,128)(2,1)}), bf16[16,128,128]{2,1,0:T(8,128)(2,1)S(1)}, u32[]{:S(2)}, u32[]{:S(2)}) async-start(bf16[16,128,128]{2,1,0:T(8,128)(2,1)} %reshape_reshape.3), calls=%async_computation.2 | async-start | bytes 1048576 | tf_op jit(solution)/shard_map/all_to_all | solution.py:17
  123.6 10.9 %all-to-all-start.5 = ((bf16[16,24,128]{2,1,0:T(8,128)(2,1)}), bf16[16,24,128]{2,1,0:T(8,128)(2,1)S(1)}, u32[]{:S(2)}, u32[]{:S(2)}) async-start(bf16[16,24,128]{2,1,0:T(8,128)(2,1)} %maximum_bitcast_fusion.1), calls=%async_computation.5 | async-start | bytes 196608 | tf_op jit(solution)/shard_map/all_to_all | solution.py:17

commit v4 on v3

--- a/solution.py
+++ b/solution.py
@@ -1,6 +1,8 @@
 import jax
 import jax.numpy as jnp
 from jax import lax
+from jax.experimental import pallas as pl
+from jax.experimental.pallas import tpu as pltpu
 from jax.sharding import Mesh, PartitionSpec as P
 
 ROW = ("y", "zq", "zp", "xl")
@@ -17,9 +19,29 @@
     return lax.all_to_all(flat, axes, split_axis=0, concat_axis=0, tiled=True).reshape(array.shape)
 
 
-def split(array):
-    high = lax.reduce_precision(array, 8, 7)
-    return jnp.concatenate([high.astype(jnp.bfloat16), (array - high).astype(jnp.bfloat16)])
+def add_up(terms):
+    total = terms[0].astype(jnp.float32)
+    for index in range(1, terms.shape[0]):
+        total = total + terms[index].astype(jnp.float32)
+    return total
+
+
+def sum_kernel(parts_ref, out_ref):
+    sums = parts_ref[0].astype(jnp.float32)
+    for index in range(1, NQ):
+        sums = sums + parts_ref[index].astype(jnp.float32)
+    sums = sums.reshape(NM + 2, CUT, sums.shape[-1])
+    shared = jnp.broadcast_to(sums[None, NM:], (NM, 2) + sums.shape[1:])
+    packed = jnp.concatenate([sums[:NM, None], shared], axis=1)
+    out_ref[...] = packed.reshape(out_ref.shape).astype(out_ref.dtype)
+
+
+def unpack_kernel(parts_ref, weight_ref, features_ref):
+    width = parts_ref.shape[-1]
+    parts = parts_ref[...].astype(jnp.float32).reshape(NM, 3, CUT, width)
+    features_ref[...] = parts[:, 0].reshape(TILE, width)
+    weight_ref[:, :width] = parts[:, 1].reshape(TILE, width)
+    weight_ref[:, width:] = parts[:, 2].reshape(TILE, width)
 
 
 def body(features, weight, upstream, tile_owners, tile_counts, tile_values):
@@ -49,14 +71,9 @@
     wanted = jnp.dot(pick, table, preferred_element_type=f32).astype(bf16)
     third = exchange(wanted.reshape(NM, total, CUT, width), NEAR)
     picked = third.transpose(1, 0, 2, 3).reshape(blocks, slots, TILE, width)
-    partial_value = jnp.einsum("btij,btjf->bif", values, picked, preferred_element_type=f32)
-
-    pair = lax.all_gather(split(partial_value), "c", axis=0).reshape(2, 2, 2, 2, TILE, width)
-    own_half = lax.dynamic_index_in_dim(pair, lax.axis_index("c"), 3, keepdims=False)
-    half_sum = jnp.sum(own_half.astype(f32), axis=(0, 1))
-    far = lax.all_gather(split(half_sum), "xh", axis=0)
-    half_total = jnp.sum(far.reshape(2, 2, 2, TILE, width).astype(f32), axis=(0, 1)).astype(bf16)
-    aggregated = lax.all_gather(half_total, "c", axis=1).reshape(blocks * TILE, width)
+    partial_value = jnp.einsum("btij,btjf->bif", values, picked, preferred_element_type=f32).astype(bf16)
+    shared = lax.all_gather(partial_value, REP, axis=0)
+    aggregated = add_up(shared).astype(bf16).reshape(blocks * TILE, width)
     upstream_all = upstream_all.transpose(0, 1, 3, 2, 4).reshape(blocks * TILE, 2 * width)
 
     pre_act = jnp.dot(aggregated, weight, preferred_element_type=f32)
@@ -71,19 +88,36 @@
     weight_cut = weight_part.astype(bf16).reshape(NM, CUT, 2, width).transpose(0, 2, 1, 3)
     fifth = exchange(jnp.concatenate([parts, weight_cut], axis=1), NEAR)
     summed = jnp.dot(pick.T, fifth[:, :total].reshape(NM * total, CUT * width), preferred_element_type=f32).astype(bf16)
-    weight_sum = jnp.sum(fifth[:, total:].astype(f32), axis=0).astype(bf16)
+    weight_sum = add_up(fifth[:, total:]).astype(bf16)
     sixth = exchange(
         jnp.concatenate(
-            [summed.reshape(NM, NQ, CUT, width).transpose(1, 0, 2, 3), jnp.broadcast_to(weight_sum[None], (NQ, 2, CUT, width))], axis=1
-        ),
+            [
+                summed.reshape(NM, NQ, CUT, width).transpose(1, 0, 2, 3),
+                jnp.broadcast_to(weight_sum[None], (NQ, 2, CUT, width)),
+            ],
+            axis=1,
+        ).reshape(NQ, (NM + 2) * CUT, width),
         "zq",
     )
-    sums = jnp.sum(sixth.astype(f32), axis=0).astype(bf16)
-    last = exchange(
-        jnp.concatenate([sums[:NM, None], jnp.broadcast_to(sums[None, NM:], (NM, 2, CUT, width))], axis=1), NEAR
-    ).astype(f32)
-    grad_features = last[:, 0].reshape(TILE, width)
-    grad_weight = last[:, 1:].transpose(0, 2, 1, 3).reshape(TILE, 2 * width)
+    near = pl.BlockSpec(memory_space=pltpu.VMEM)
+    room = pltpu.CompilerParams(vmem_limit_bytes=4 * 1024 * 1024)
+    packed = pl.pallas_call(
+        sum_kernel,
+        out_shape=jax.ShapeDtypeStruct((NM, 3 * CUT, width), bf16),
+        in_specs=[near],
+        out_specs=near,
+        compiler_params=room,
+        name="sum_far",
+    )(sixth)
+    last = exchange(packed, NEAR)
+    grad_weight, grad_features = pl.pallas_call(
+        unpack_kernel,
+        out_shape=(jax.ShapeDtypeStruct((TILE, 2 * width), f32), jax.ShapeDtypeStruct((TILE, width), f32)),
+        in_specs=[near],
+        out_specs=(near, near),
+        compiler_params=room,
+        name="unpack",
+    )(last)
     return (hidden, grad_weight, grad_features)
 
 

time: 137 us -> 132 us (0.964)
  blocking collectives: 61.1 us -> 57.7 us
  local copies, waits for them, and re-layouts: 6.94 us -> 5.27 us
  Pallas kernels: 0 us -> 1.37 us
    all_gather x3 -> x1, blocking collectives: 11.8 us -> 8.02 us  [body(): shared = lax.all_gather(partial_value, REP, axis=0)]
    pallas_call x0 -> x2, Pallas kernels: none -> 1.37 us  [the longest x1 0.69 us: body(): pl.pallas_call(unpack_kernel, out_shape=(jax.ShapeDtypeStruct((TILE, 2 *...]
where the time goes in v4:
time: 132 us; the launch traced here: 131 us
  blocking collectives  57.7 us (44%)
  waiting for transfers between devices  33.5 us (25%)
  starting transfers between devices  27.7 us (21%)
  local copies, waits for them, and re-layouts  5.27 us (4%)
  other arithmetic  2.51 us (2%)
  matrix products  2.24 us (2%)
  Pallas kernels  1.37 us (1%)
    all_to_all x2, blocking collectives, exchange(): lax.all_to_all(flat, axes, split_axis=0, concat_axis=0, tiled=True)  41.2 us
    all_to_all x4, waiting for transfers between devices, exchange(): lax.all_to_all(flat, axes, split_axis=0, concat_axis=0, tiled=True)  33.5 us
    all_to_all x4, starting transfers between devices, exchange(): lax.all_to_all(flat, axes, split_axis=0, concat_axis=0, tiled=True)  27.7 us
    all_gather x1, blocking collectives, body(): shared = lax.all_gather(partial_value, REP, axis=0)  8.02 us
    all_gather x1, blocking collectives, body(): lax.all_gather(halves, 'xh', axis=0)  6.45 us
  transfers between devices with their start and end apart: 4, of which 4 were waited for; matrix products, arithmetic and copies ran while one was open for 2% of the time, Pallas kernels for 0%

profile of v4, /device:TPU:4, one launch (start us, length us, event | category | flops | bytes accessed | tf_op | source)
XLA Modules:
  0.0 131.2 jit_solution(15868542886155627906)
XLA Ops:
  0.6 1.5 %broadcast_in_dim.12 = bf16[8,128,128]{2,1,0:T(8,128)(2,1)} broadcast(bf16[128,128]{1,0:T(8,128)(2,1)} %param.6), dimensions={1,2} | broadcast | bytes 294912 | tf_op jit(solution)/shard_map/broadcast_in_dim | solution.py:56
  2.2 15.2 %all-to-all-start = ((bf16[8,128,128]{2,1,0:T(8,128)(2,1)}), bf16[8,128,128]{2,1,0:T(8,128)(2,1)S(1)}, u32[]{:S(2)}, u32[]{:S(2)}) async-start(bf16[8,128,128]{2,1,0:T(8,128)(2,1)} %broadcast_in_dim.12), calls=%async_computation | async-start | bytes 524288 | tf_op jit(solution)/shard_map/all_to_all | solution.py:19
  17.4 0.7 copy-done.4
  18.2 0.5 broadcast.157
  18.8 0.7 reduce.7
  19.6 6.4 %all-gather = bf16[4,128,128]{2,1,0:T(8,128)(2,1)S(1)} all-gather(bf16[2,128,128]{2,1,0:T(8,128)(2,1)S(1)} %pad_maximum_fusion.1), channel_id=2, replica_groups=mesh['y'=4,'zq'=8,'zp'=2,'xl'=2,'xh'=2,'c'=2] {'xh'}, dimensions={0}, use_global_device_ids=true | all-gather | bytes 196608 | tf_op jit(solution)/shard_map/all_gather | solution.py:60
  26.1 2.0 %all-gather.1 = bf16[2,4,128,128]{3,2,1,0:T(8,128)(2,1)S(1)} all-gather(bf16[2,2,128,128]{3,2,1,0:T(8,128)(2,1)S(1)} %bitcast.111), channel_id=3, replica_groups=mesh['y'=4,'zq'=8,'zp'=2,'xl'=2,'xh'=2,'c'=2] {'c'}, dimensions={1}, use_global_device_ids=true | all-gather | bytes 393216 | tf_op jit(solution)/shard_map/all_gather | solution.py:60
  28.1 10.7 %all-to-all-done = bf16[8,128,128]{2,1,0:T(8,128)(2,1)S(1)} async-done(((bf16[8,128,128]{2,1,0:T(8,128)(2,1)}), bf16[8,128,128]{2,1,0:T(8,128)(2,1)S(1)}, u32[]{:S(2)}, u32[]{:S(2)}) %all-to-all-start) | async-done | bytes 262176 | tf_op jit(solution)/shard_map/all_to_all | solution.py:19
  38.8 0.8 copy_bitcast_fusion.1
  39.5 5.2 %all-to-all-start.1 = ((bf16[16,72,128]{2,1,0:T(8,128)(2,1)}), bf16[16,72,128]{2,1,0:T(8,128)(2,1)S(1)}, u32[]{:S(2)}, u32[]{:S(2)}) async-start(bf16[16,72,128]{2,1,0:T(8,128)(2,1)} %copy_bitcast_fusion.1), calls=%async_computation.1 | async-start | bytes 589824 | tf_op jit(solution)/shard_map/all_to_all | solution.py:19
  44.8 8.0 %all-to-all-done.1 = bf16[16,72,128]{2,1,0:T(8,128)(2,1)S(1)} async-done(((bf16[16,72,128]{2,1,0:T(8,128)(2,1)}), bf16[16,72,128]{2,1,0:T(8,128)(2,1)S(1)}, u32[]{:S(2)}, u32[]{:S(2)}) %all-to-all-start.1) | async-done | bytes 294944 | tf_op jit(solution)/shard_map/all_to_all | solution.py:19
  53.0 0.3 convolution_convert_fusion
  53.3 1.0 reshape_reshape.3
  54.3 3.7 %all-to-all-start.2 = ((bf16[16,128,128]{2,1,0:T(8,128)(2,1)}), bf16[16,128,128]{2,1,0:T(8,128)(2,1)S(1)}, u32[]{:S(2)}, u32[]{:S(2)}) async-start(bf16[16,128,128]{2,1,0:T(8,128)(2,1)} %reshape_reshape.3), calls=%async_computation.2 | async-start | bytes 1048576 | tf_op jit(solution)/shard_map/all_to_all | solution.py:19
  58.0 0.3 copy.32
  58.4 0.4 copy.31
  58.8 8.1 %all-to-all-done.2 = bf16[16,128,128]{2,1,0:T(8,128)(2,1)S(1)} async-done(((bf16[16,128,128]{2,1,0:T(8,128)(2,1)}), bf16[16,128,128]{2,1,0:T(8,128)(2,1)S(1)}, u32[]{:S(2)}, u32[]{:S(2)}) %all-to-all-start.2) | async-done | bytes 524320 | tf_op jit(solution)/shard_map/all_to_all | solution.py:19
  67.1 0.3 fusion.2
  67.4 0.1 copy.30
  67.5 8.0 %all-gather.2 = bf16[16,128,128]{2,1,0:T(8,128)(2,1)S(1)} all-gather(bf16[4,128,128]{2,1,0:T(8,128)(2,1)S(1)} %copy.30), channel_id=4, replica_groups=mesh['y'=4,'zq'=8,'zp'=2,'xl'=2,'xh'=2,'c'=2] {'xh','c'}, dimensions={0}, use_global_device_ids=true | all-gather | bytes 655360 | tf_op jit(solution)/shard_map/all_gather | solution.py:75
  75.7 0.5 fusion.10
  76.2 0.2 fusion.3
  76.4 0.2 convolution_convert_fusion.2
  76.6 0.3 fusion.31
  77.2 15.5 %all_to_all.30 = bf16[16,144,128]{2,1,0:T(8,128)(2,1)S(1)} all-to-all(bf16[16,144,128]{2,1,0:T(8,128)(2,1)S(1)} %maximum_bitcast_fusion), channel_id=1, replica_groups=mesh['y'=4,'zq'=8,'zp'=2,'xl'=2,'xh'=2,'c'=2] {'y','zp','xl'}, dimensions={0} | all-to-all | bytes 1179648 | tf_op jit(solution)/shard_map/all_to_all | solution.py:19
  92.8 0.3 fusion
  93.2 25.7 %all_to_all.31.parts_ref = bf16[8,144,128]{2,1,0:T(8,128)(2,1)S(1)} all-to-all(bf16[8,144,128]{2,1,0:T(8,128)(2,1)S(1)} %maximum_bitcast_fusion.1), channel_id=1, replica_groups=mesh['y'=4,'zq'=8,'zp'=2,'xl'=2,'xh'=2,'c'=2] {'zq'}, dimensions={0} | all-to-all | bytes 589824 | tf_op jit(solution)/shard_map/all_to_all | solution.py:19
  118.9 0.7 sum_far.1
  119.6 3.6 %all-to-all-start.5 = ((bf16[16,24,128]{2,1,0:T(8,128)(2,1)}), bf16[16,24,128]{2,1,0:T(8,128)(2,1)S(1)}, u32[]{:S(2)}, u32[]{:S(2)}) async-start(bf16[16,24,128]{2,1,0:T(8,128)(2,1)} %sum_far.1), calls=%async_computation.5 | async-start | bytes 196608 | tf_op jit(solution)/shard_map/all_to_all | solution.py:19
  123.2 0.7 fusion.20
  123.9 6.6 %all-to-all-done.5.parts_ref = bf16[16,24,128]{2,1,0:T(8,128)(2,1)S(1)} async-done(((bf16[16,24,128]{2,1,0:T(8,128)(2,1)}), bf16[16,24,128]{2,1,0:T(8,128)(2,1)S(1)}, u32[]{:S(2)}, u32[]{:S(2)}) %all-to-all-start.5) | async-done | bytes 98336 | tf_op jit(solution)/shard_map/all_to_all | solution.py:19
  130.5 0.7 unpack.1
  (32 shorter events, 1.2 us)
Async XLA Ops:
  0.6 75.0 %copy-start = (bf16[128,256]{1,0:T(8,128)(2,1)S(1)}, bf16[128,256]{1,0:T(8,128)(2,1)}, u32[]{:S(2)}) copy-start(bf16[128,256]{1,0:T(8,128)(2,1)} %param.7) | copy-start | bytes 196612
  2.2 17.4 %copy-start.2 = (bf16[128,256]{1,0:T(8,128)(2,1)S(1)}, bf16[128,256]{1,0:T(8,128)(2,1)}, u32[]{:S(2)}) copy-start(bf16[128,256]{1,0:T(8,128)(2,1)} %param.8) | copy-start | bytes 196612
  2.2 36.6 %all-to-all-start = ((bf16[8,128,128]{2,1,0:T(8,128)(2,1)}), bf16[8,128,128]{2,1,0:T(8,128)(2,1)S(1)}, u32[]{:S(2)}, u32[]{:S(2)}) async-start(bf16[8,128,128]{2,1,0:T(8,128)(2,1)} %broadcast_in_dim.12), calls=%async_computation | async-start | bytes 524288 | tf_op jit(solution)/shard_map/all_to_all | solution.py:19
  17.4 0.7 copy-start.4
  18.1 0.7 copy-start.3
  39.5 13.3 %all-to-all-start.1 = ((bf16[16,72,128]{2,1,0:T(8,128)(2,1)}), bf16[16,72,128]{2,1,0:T(8,128)(2,1)S(1)}, u32[]{:S(2)}, u32[]{:S(2)}) async-start(bf16[16,72,128]{2,1,0:T(8,128)(2,1)} %copy_bitcast_fusion.1), calls=%async_computation.1 | async-start | bytes 589824 | tf_op jit(solution)/shard_map/all_to_all | solution.py:19
  54.3 3.7 %copy-start.1 = (bf16[4,1,4,128,128]{4,3,2,1,0:T(8,128)(2,1)S(1)}, bf16[4,1,4,128,128]{4,3,2,1,0:T(8,128)(2,1)}, u32[]{:S(2)}) copy-start(bf16[4,1,4,128,128]{4,3,2,1,0:T(8,128)(2,1)} %param.11) | copy-start | bytes 1572868
  54.3 12.6 %all-to-all-start.2 = ((bf16[16,128,128]{2,1,0:T(8,128)(2,1)}), bf16[16,128,128]{2,1,0:T(8,128)(2,1)S(1)}, u32[]{:S(2)}, u32[]{:S(2)}) async-start(bf16[16,128,128]{2,1,0:T(8,128)(2,1)} %reshape_reshape.3), calls=%async_computation.2 | async-start | bytes 1048576 | tf_op jit(solution)/shard_map/all_to_all | solution.py:19
  119.6 10.9 %all-to-all-start.5 = ((bf16[16,24,128]{2,1,0:T(8,128)(2,1)}), bf16[16,24,128]{2,1,0:T(8,128)(2,1)S(1)}, u32[]{:S(2)}, u32[]{:S(2)}) async-start(bf16[16,24,128]{2,1,0:T(8,128)(2,1)} %sum_far.1), calls=%async_computation.5 | async-start | bytes 196608 | tf_op jit(solution)/shard_map/all_to_all | solution.py:19

commit v5 on v4

--- a/solution.py
+++ b/solution.py
@@ -26,6 +26,20 @@
     return total
 
 
+def start_kernel(features_ref, owners_ref, counts_ref, out_ref):
+    width = features_ref.shape[1]
+    blocks, slots = owners_ref.shape
+    lane = lax.broadcasted_iota(jnp.int32, (CUT, width), 1)
+    code = jnp.full((CUT, width), -1, jnp.int32)
+    for block in range(blocks):
+        for slot in range(slots):
+            wanted = jnp.where(slot < counts_ref[0, block], owners_ref[block, slot], -1)
+            code = jnp.where(lane == block * slots + slot, wanted, code)
+    code = jnp.broadcast_to(code.astype(jnp.float32)[None], (NM, CUT, width))
+    cut = features_ref[...].astype(jnp.float32).reshape(NM, CUT, width)
+    out_ref[...] = jnp.concatenate([cut, code], axis=1).astype(out_ref.dtype)
+
+
 def sum_kernel(parts_ref, out_ref):
     sums = parts_ref[0].astype(jnp.float32)
     for index in range(1, NQ):
@@ -47,27 +61,33 @@
 def body(features, weight, upstream, tile_owners, tile_counts, tile_values):
     f32, bf16 = jnp.float32, jnp.bfloat16
     width = features.shape[1]
-    owners = tile_owners[:, 0, :]
-    counts = tile_counts[:, 0]
     values = tile_values[:, 0]
-    blocks, slots = owners.shape
+    blocks, slots = values.shape[:2]
     total = blocks * slots
-    active = jnp.arange(slots, dtype=jnp.int32)[None, :] < counts[:, None]
-    wide = exchange(jnp.broadcast_to(features[None], (NQ, TILE, width)), "zq")
-    code = jnp.where(active, owners, -1).reshape(total).astype(bf16)
-    code_rows = jnp.broadcast_to(jnp.pad(code, (0, width - total))[None, None, None, :], (NM, 1, CUT, width))
+    near = pl.BlockSpec(memory_space=pltpu.VMEM)
+    scalar = pl.BlockSpec(memory_space=pltpu.SMEM)
+    room = pltpu.CompilerParams(vmem_limit_bytes=4 * 1024 * 1024)
+
+    start = pl.pallas_call(
+        start_kernel,
+        out_shape=jax.ShapeDtypeStruct((NM, 2 * CUT, width), bf16),
+        in_specs=[near, scalar, scalar],
+        out_specs=near,
+        compiler_params=room,
+        name="start",
+    )(features, tile_owners.reshape(blocks, slots), tile_counts.reshape(1, blocks))
+    first = exchange(start, NEAR)
+    spread = jnp.broadcast_to(first[None, :, :CUT], (NQ, NM, CUT, width)).reshape(NQ, NM * CUT, width)
+    table = exchange(spread, "zq")
+    codes = first[:, CUT, :total].astype(jnp.int32).reshape(NM * total)
+    place = jnp.arange(NQ * NM, dtype=jnp.int32)
+    ident = ((place // (NZP * NX)) % NY) * (NQ * NZP * NX) + (place // NM) * (NZP * NX) + place % (NZP * NX)
+    pick = (codes[:, None] == ident[None, :]).astype(bf16)
     halves = jnp.stack([upstream[:, :width], upstream[:, width:]])
+    first, halves = lax.optimization_barrier((first, halves))
     upstream_all = lax.all_gather(lax.all_gather(halves, "xh", axis=0), "c", axis=1)
-    wide, code_rows, upstream_all = lax.optimization_barrier((wide, code_rows, upstream_all))
-
-    slices = wide.reshape(NQ, NM, CUT, width).transpose(1, 0, 2, 3)
-    second = exchange(jnp.concatenate([slices, code_rows], axis=1), NEAR)
-    codes = second[:, NQ, 0, :total].astype(jnp.int32).reshape(NM * total)
-    place = jnp.arange(NQ * NM, dtype=jnp.int32)
-    member = place // NQ
-    ident = (member // (NZP * NX)) * (NQ * NZP * NX) + (place % NQ) * (NZP * NX) + member % (NZP * NX)
-    pick = (codes[:, None] == ident[None, :]).astype(bf16)
-    table = second[:, :NQ].reshape(NQ * NM, CUT * width)
+    table, upstream_all, pick = lax.optimization_barrier((table, upstream_all, pick))
+    table = table.reshape(NQ * NM, CUT * width)
     wanted = jnp.dot(pick, table, preferred_element_type=f32).astype(bf16)
     third = exchange(wanted.reshape(NM, total, CUT, width), NEAR)
     picked = third.transpose(1, 0, 2, 3).reshape(blocks, slots, TILE, width)
@@ -92,15 +112,13 @@
     sixth = exchange(
         jnp.concatenate(
             [
-                summed.reshape(NM, NQ, CUT, width).transpose(1, 0, 2, 3),
+                summed.reshape(NQ, NM, CUT, width),
                 jnp.broadcast_to(weight_sum[None], (NQ, 2, CUT, width)),
             ],
             axis=1,
         ).reshape(NQ, (NM + 2) * CUT, width),
         "zq",
     )
-    near = pl.BlockSpec(memory_space=pltpu.VMEM)
-    room = pltpu.CompilerParams(vmem_limit_bytes=4 * 1024 * 1024)
     packed = pl.pallas_call(
         sum_kernel,
         out_shape=jax.ShapeDtypeStruct((NM, 3 * CUT, width), bf16),

time: 132 us -> 130 us (0.985)
  blocking collectives: 57.7 us -> 71.1 us
  waiting for transfers between devices: 33.5 us -> 26 us
  starting transfers between devices: 27.7 us -> 21.6 us
  other arithmetic: 2.51 us -> 1.1 us
    all_to_all x2 -> x3, blocking collectives: 41.2 us -> 54.7 us  [exchange(): lax.all_to_all(flat, axes, split_axis=0, concat_axis=0, tiled=True)]
    all_to_all x4 -> x3, waiting for transfers between devices: 33.5 us -> 26 us  [exchange(): lax.all_to_all(flat, axes, split_axis=0, concat_axis=0, tiled=True)]
    all_to_all x4 -> x3, starting transfers between devices: 27.7 us -> 21.6 us  [exchange(): lax.all_to_all(flat, axes, split_axis=0, concat_axis=0, tiled=True)]
  transfers between devices with their start and end apart: 4 -> 3, of which waited for: 4 -> 3; matrix products, arithmetic and copies ran while one was open for 2% -> 1% of each run, Pallas kernels for 0% -> 0%
where the time goes in v5:
time: 130 us; the launch traced here: 129 us
  blocking collectives  71.1 us (55%)
  waiting for transfers between devices  26 us (20%)
  starting transfers between devices  21.6 us (17%)
  local copies, waits for them, and re-layouts  4.62 us (4%)
  matrix products  2.09 us (2%)
  Pallas kernels  1.96 us (2%)
    all_to_all x3, blocking collectives, exchange(): lax.all_to_all(flat, axes, split_axis=0, concat_axis=0, tiled=True)  54.7 us
    all_to_all x3, waiting for transfers between devices, exchange(): lax.all_to_all(flat, axes, split_axis=0, concat_axis=0, tiled=True)  26 us
    all_to_all x3, starting transfers between devices, exchange(): lax.all_to_all(flat, axes, split_axis=0, concat_axis=0, tiled=True)  21.6 us
    all_gather x1, blocking collectives, body(): shared = lax.all_gather(partial_value, REP, axis=0)  8.02 us
    all_gather x1, blocking collectives, body(): lax.all_gather(halves, 'xh', axis=0)  6.44 us
  transfers between devices with their start and end apart: 3, of which 3 were waited for; matrix products, arithmetic and copies ran while one was open for 1% of the time, Pallas kernels for 0%

profile of v5, /device:TPU:4, one launch (start us, length us, event | category | flops | bytes accessed | tf_op | source)
XLA Modules:
  0.0 129.4 jit_solution(4318432694060923385)
XLA Ops:
  0.7 0.7 copy-done.2
  1.4 0.8 copy-done.1
  2.1 0.6 start.1
  2.7 13.6 %all_to_all.30 = bf16[16,16,128]{2,1,0:T(8,128)(2,1)S(1)} all-to-all(bf16[16,16,128]{2,1,0:T(8,128)(2,1)S(1)} %start.1), channel_id=1, replica_groups=mesh['y'=4,'zq'=8,'zp'=2,'xl'=2,'xh'=2,'c'=2] {'y','zp','xl'}, dimensions={0} | all-to-all | bytes 131072 | tf_op jit(solution)/shard_map/all_to_all | solution.py:19
  16.3 0.7 broadcast_in_dim.18
  17.0 14.3 %all-to-all-start.1 = ((bf16[8,128,128]{2,1,0:T(8,128)(2,1)}), bf16[8,128,128]{2,1,0:T(8,128)(2,1)S(1)}, u32[]{:S(2)}, u32[]{:S(2)}) async-start(bf16[8,128,128]{2,1,0:T(8,128)(2,1)} %broadcast_in_dim.18), calls=%async_computation.1 | async-start | bytes 524288 | tf_op jit(solution)/shard_map/all_to_all | solution.py:19
  31.5 6.4 %all-gather = bf16[4,128,128]{2,1,0:T(8,128)(2,1)S(1)} all-gather(bf16[2,128,128]{2,1,0:T(8,128)(2,1)S(1)} %pad_maximum_fusion), channel_id=2, replica_groups=mesh['y'=4,'zq'=8,'zp'=2,'xl'=2,'xh'=2,'c'=2] {'xh'}, dimensions={0}, use_global_device_ids=true | all-gather | bytes 196608 | tf_op jit(solution)/shard_map/all_gather | solution.py:88
  38.0 2.0 %all-gather.1 = bf16[2,4,128,128]{3,2,1,0:T(8,128)(2,1)S(1)} all-gather(bf16[2,2,128,128]{3,2,1,0:T(8,128)(2,1)S(1)} %bitcast.103), channel_id=3, replica_groups=mesh['y'=4,'zq'=8,'zp'=2,'xl'=2,'xh'=2,'c'=2] {'c'}, dimensions={1}, use_global_device_ids=true | all-gather | bytes 393216 | tf_op jit(solution)/shard_map/all_gather | solution.py:88
  40.0 11.2 %all-to-all-done.1 = bf16[8,128,128]{2,1,0:T(8,128)(2,1)S(1)} async-done(((bf16[8,128,128]{2,1,0:T(8,128)(2,1)}), bf16[8,128,128]{2,1,0:T(8,128)(2,1)S(1)}, u32[]{:S(2)}, u32[]{:S(2)}) %all-to-all-start.1) | async-done | bytes 262176 | tf_op jit(solution)/shard_map/all_to_all | solution.py:19
  51.4 0.3 convolution_convert_fusion
  51.7 1.0 reshape_reshape.3
  52.7 3.7 %all-to-all-start.2 = ((bf16[16,128,128]{2,1,0:T(8,128)(2,1)}), bf16[16,128,128]{2,1,0:T(8,128)(2,1)S(1)}, u32[]{:S(2)}, u32[]{:S(2)}) async-start(bf16[16,128,128]{2,1,0:T(8,128)(2,1)} %reshape_reshape.3), calls=%async_computation.2 | async-start | bytes 1048576 | tf_op jit(solution)/shard_map/all_to_all | solution.py:19
  56.4 0.3 copy.27
  56.7 0.4 copy.26
  57.2 8.1 %all-to-all-done.2 = bf16[16,128,128]{2,1,0:T(8,128)(2,1)S(1)} async-done(((bf16[16,128,128]{2,1,0:T(8,128)(2,1)}), bf16[16,128,128]{2,1,0:T(8,128)(2,1)S(1)}, u32[]{:S(2)}, u32[]{:S(2)}) %all-to-all-start.2) | async-done | bytes 524320 | tf_op jit(solution)/shard_map/all_to_all | solution.py:19
  65.3 0.1 copy.23
  65.4 0.3 fusion.2
  65.8 0.1 copy.25
  65.9 8.0 %all-gather.2 = bf16[16,128,128]{2,1,0:T(8,128)(2,1)S(1)} all-gather(bf16[4,128,128]{2,1,0:T(8,128)(2,1)S(1)} %copy.25), channel_id=4, replica_groups=mesh['y'=4,'zq'=8,'zp'=2,'xl'=2,'xh'=2,'c'=2] {'xh','c'}, dimensions={0}, use_global_device_ids=true | all-gather | bytes 655360 | tf_op jit(solution)/shard_map/all_gather | solution.py:95
  74.0 0.5 fusion.10
  74.5 0.2 fusion.3
  74.8 0.2 convolution_convert_fusion.2
  75.0 0.3 fusion.25
  75.4 0.1 copy.40
  75.6 15.5 %all_to_all.31 = bf16[16,144,128]{2,1,0:T(8,128)(2,1)S(1)} all-to-all(bf16[16,144,128]{2,1,0:T(8,128)(2,1)S(1)} %maximum_bitcast_fusion), channel_id=1, replica_groups=mesh['y'=4,'zq'=8,'zp'=2,'xl'=2,'xh'=2,'c'=2] {'y','zp','xl'}, dimensions={0} | all-to-all | bytes 1179648 | tf_op jit(solution)/shard_map/all_to_all | solution.py:19
  91.2 0.2 fusion
  91.5 25.6 %all_to_all.32.parts_ref = bf16[8,144,128]{2,1,0:T(8,128)(2,1)S(1)} all-to-all(bf16[8,144,128]{2,1,0:T(8,128)(2,1)S(1)} %maximum_bitcast_fusion.1), channel_id=1, replica_groups=mesh['y'=4,'zq'=8,'zp'=2,'xl'=2,'xh'=2,'c'=2] {'zq'}, dimensions={0} | all-to-all | bytes 589824 | tf_op jit(solution)/shard_map/all_to_all | solution.py:19
  117.1 0.7 sum_far.1
  117.8 3.6 %all-to-all-start.5 = ((bf16[16,24,128]{2,1,0:T(8,128)(2,1)}), bf16[16,24,128]{2,1,0:T(8,128)(2,1)S(1)}, u32[]{:S(2)}, u32[]{:S(2)}) async-start(bf16[16,24,128]{2,1,0:T(8,128)(2,1)} %sum_far.1), calls=%async_computation.5 | async-start | bytes 196608 | tf_op jit(solution)/shard_map/all_to_all | solution.py:19
  121.4 0.7 fusion.16
  122.1 6.6 %all-to-all-done.5.parts_ref = bf16[16,24,128]{2,1,0:T(8,128)(2,1)S(1)} async-done(((bf16[16,24,128]{2,1,0:T(8,128)(2,1)}), bf16[16,24,128]{2,1,0:T(8,128)(2,1)S(1)}, u32[]{:S(2)}, u32[]{:S(2)}) %all-to-all-start.5) | async-done | bytes 98336 | tf_op jit(solution)/shard_map/all_to_all | solution.py:19
  128.7 0.7 unpack.1
  (27 shorter events, 0.8 us)
Async XLA Ops:
  0.6 73.4 %copy-start = (bf16[128,256]{1,0:T(8,128)(2,1)S(1)}, bf16[128,256]{1,0:T(8,128)(2,1)}, u32[]{:S(2)}) copy-start(bf16[128,256]{1,0:T(8,128)(2,1)} %param.7) | copy-start | bytes 196612
  0.6 0.7 copy-start.2
  0.7 0.7 copy-start.3
  1.4 0.8 copy-start.1
  17.0 14.3 %copy-start.5 = (bf16[128,256]{1,0:T(8,128)(2,1)S(1)}, bf16[128,256]{1,0:T(8,128)(2,1)}, u32[]{:S(2)}) copy-start(bf16[128,256]{1,0:T(8,128)(2,1)} %param.8) | copy-start | bytes 196612
  17.0 34.2 %all-to-all-start.1 = ((bf16[8,128,128]{2,1,0:T(8,128)(2,1)}), bf16[8,128,128]{2,1,0:T(8,128)(2,1)S(1)}, u32[]{:S(2)}, u32[]{:S(2)}) async-start(bf16[8,128,128]{2,1,0:T(8,128)(2,1)} %broadcast_in_dim.18), calls=%async_computation.1 | async-start | bytes 524288 | tf_op jit(solution)/shard_map/all_to_all | solution.py:19
  52.7 3.7 %copy-start.4 = (bf16[4,1,4,128,128]{4,3,2,1,0:T(8,128)(2,1)S(1)}, bf16[4,1,4,128,128]{4,3,2,1,0:T(8,128)(2,1)}, u32[]{:S(2)}) copy-start(bf16[4,1,4,128,128]{4,3,2,1,0:T(8,128)(2,1)} %param.11) | copy-start | bytes 1572868
  52.7 12.6 %all-to-all-start.2 = ((bf16[16,128,128]{2,1,0:T(8,128)(2,1)}), bf16[16,128,128]{2,1,0:T(8,128)(2,1)S(1)}, u32[]{:S(2)}, u32[]{:S(2)}) async-start(bf16[16,128,128]{2,1,0:T(8,128)(2,1)} %reshape_reshape.3), calls=%async_computation.2 | async-start | bytes 1048576 | tf_op jit(solution)/shard_map/all_to_all | solution.py:19
  117.8 10.9 %all-to-all-start.5 = ((bf16[16,24,128]{2,1,0:T(8,128)(2,1)}), bf16[16,24,128]{2,1,0:T(8,128)(2,1)S(1)}, u32[]{:S(2)}, u32[]{:S(2)}) async-start(bf16[16,24,128]{2,1,0:T(8,128)(2,1)} %sum_far.1), calls=%async_computation.5 | async-start | bytes 196608 | tf_op jit(solution)/shard_map/all_to_all | solution.py:19

commit v6 on v5

--- a/solution.py
+++ b/solution.py
@@ -14,9 +14,13 @@
 CUT = TILE // NM
 
 
-def exchange(array, axes):
+ORDER = [(index + NQ // 2) % NQ for index in range(NQ)]
+
+
+def exchange(array, axes, groups=None):
     flat = array.reshape(array.shape[0], -1, array.shape[-1])
-    return lax.all_to_all(flat, axes, split_axis=0, concat_axis=0, tiled=True).reshape(array.shape)
+    flat = lax.all_to_all(flat, axes, split_axis=0, concat_axis=0, axis_index_groups=groups, tiled=True)
+    return flat.reshape(array.shape)
 
 
 def add_up(terms):
@@ -78,10 +82,10 @@
     )(features, tile_owners.reshape(blocks, slots), tile_counts.reshape(1, blocks))
     first = exchange(start, NEAR)
     spread = jnp.broadcast_to(first[None, :, :CUT], (NQ, NM, CUT, width)).reshape(NQ, NM * CUT, width)
-    table = exchange(spread, "zq")
+    table = exchange(spread, "zq", [ORDER])
     codes = first[:, CUT, :total].astype(jnp.int32).reshape(NM * total)
     place = jnp.arange(NQ * NM, dtype=jnp.int32)
-    ident = ((place // (NZP * NX)) % NY) * (NQ * NZP * NX) + (place // NM) * (NZP * NX) + place % (NZP * NX)
+    ident = ((place // (NZP * NX)) % NY) * (NQ * NZP * NX) + ((place // NM + NQ // 2) % NQ) * (NZP * NX) + place % (NZP * NX)
     pick = (codes[:, None] == ident[None, :]).astype(bf16)
     halves = jnp.stack([upstream[:, :width], upstream[:, width:]])
     first, halves = lax.optimization_barrier((first, halves))
@@ -118,6 +122,7 @@
             axis=1,
         ).reshape(NQ, (NM + 2) * CUT, width),
         "zq",
+        [ORDER],
     )
     packed = pl.pallas_call(
         sum_kernel,

time: 130 us -> 124 us (0.954)
  waiting for transfers between devices: 26 us -> 17.8 us
  starting transfers between devices: 21.6 us -> 24.8 us
  blocking collectives: 71.1 us -> 69.6 us
    all_to_all x3, waiting for transfers between devices: 26 us -> 17.8 us  [exchange(): lax.all_to_all(flat, axes, split_axis=0, concat_axis=0, axis_index_groups...]
    all_to_all x3, starting transfers between devices: 21.6 us -> 24.8 us  [exchange(): lax.all_to_all(flat, axes, split_axis=0, concat_axis=0, axis_index_groups...]
    all_to_all x3, blocking collectives: 54.7 us -> 53.1 us  [exchange(): lax.all_to_all(flat, axes, split_axis=0, concat_axis=0, axis_index_groups...]
where the time goes in v6:
time: 124 us; the launch traced here: 123 us
  blocking collectives  69.6 us (56%)
  starting transfers between devices  24.8 us (20%)
  waiting for transfers between devices  17.8 us (14%)
  local copies, waits for them, and re-layouts  4.62 us (4%)
  matrix products  2.09 us (2%)
  Pallas kernels  1.96 us (2%)
    all_to_all x3, blocking collectives, exchange(): lax.all_to_all(flat, axes, split_axis=0, concat_axis=0, axis_index_groups...  53.1 us
    all_to_all x3, starting transfers between devices, exchange(): lax.all_to_all(flat, axes, split_axis=0, concat_axis=0, axis_index_groups...  24.8 us
    all_to_all x3, waiting for transfers between devices, exchange(): lax.all_to_all(flat, axes, split_axis=0, concat_axis=0, axis_index_groups...  17.8 us
    all_gather x1, blocking collectives, body(): shared = lax.all_gather(partial_value, REP, axis=0)  8.02 us
    all_gather x1, blocking collectives, body(): lax.all_gather(halves, 'xh', axis=0)  6.44 us
  transfers between devices with their start and end apart: 3, of which 3 were waited for; matrix products, arithmetic and copies ran while one was open for 1% of the time, Pallas kernels for 0%

profile of v6, /device:TPU:4, one launch (start us, length us, event | category | flops | bytes accessed | tf_op | source)
XLA Modules:
  0.0 122.9 jit_solution(13707654308689672518)
XLA Ops:
  0.7 0.7 copy-done.2
  1.4 0.8 copy-done.1
  2.1 0.6 start.1
  2.7 13.6 %all_to_all.30 = bf16[16,16,128]{2,1,0:T(8,128)(2,1)S(1)} all-to-all(bf16[16,16,128]{2,1,0:T(8,128)(2,1)S(1)} %start.1), channel_id=1, replica_groups=mesh['y'=4,'zq'=8,'zp'=2,'xl'=2,'xh'=2,'c'=2] {'y','zp','xl'}, dimensions={0} | all-to-all | bytes 131072 | tf_op jit(solution)/shard_map/all_to_all | solution.py:22
  16.3 0.7 broadcast_in_dim.18
  17.0 17.6 %all-to-all-start.1 = ((bf16[8,128,128]{2,1,0:T(8,128)(2,1)}), bf16[8,128,128]{2,1,0:T(8,128)(2,1)S(1)}, u32[]{:S(2)}, u32[]{:S(2)}) async-start(bf16[8,128,128]{2,1,0:T(8,128)(2,1)} %broadcast_in_dim.18), calls=%async_computation.1 | async-start | bytes 524288 | tf_op jit(solution)/shard_map/all_to_all | solution.py:22
  34.8 6.4 %all-gather = bf16[4,128,128]{2,1,0:T(8,128)(2,1)S(1)} all-gather(bf16[2,128,128]{2,1,0:T(8,128)(2,1)S(1)} %pad_maximum_fusion), channel_id=2, replica_groups=mesh['y'=4,'zq'=8,'zp'=2,'xl'=2,'xh'=2,'c'=2] {'xh'}, dimensions={0}, use_global_device_ids=true | all-gather | bytes 196608 | tf_op jit(solution)/shard_map/all_gather | solution.py:92
  41.2 2.0 %all-gather.1 = bf16[2,4,128,128]{3,2,1,0:T(8,128)(2,1)S(1)} all-gather(bf16[2,2,128,128]{3,2,1,0:T(8,128)(2,1)S(1)} %bitcast.103), channel_id=3, replica_groups=mesh['y'=4,'zq'=8,'zp'=2,'xl'=2,'xh'=2,'c'=2] {'c'}, dimensions={1}, use_global_device_ids=true | all-gather | bytes 393216 | tf_op jit(solution)/shard_map/all_gather | solution.py:92
  43.3 1.7 %all-to-all-done.1 = bf16[8,128,128]{2,1,0:T(8,128)(2,1)S(1)} async-done(((bf16[8,128,128]{2,1,0:T(8,128)(2,1)}), bf16[8,128,128]{2,1,0:T(8,128)(2,1)S(1)}, u32[]{:S(2)}, u32[]{:S(2)}) %all-to-all-start.1) | async-done | bytes 262176 | tf_op jit(solution)/shard_map/all_to_all | solution.py:22
  45.1 0.3 convolution_convert_fusion
  45.4 1.0 reshape_reshape.3
  46.5 3.7 %all-to-all-start.2 = ((bf16[16,128,128]{2,1,0:T(8,128)(2,1)}), bf16[16,128,128]{2,1,0:T(8,128)(2,1)S(1)}, u32[]{:S(2)}, u32[]{:S(2)}) async-start(bf16[16,128,128]{2,1,0:T(8,128)(2,1)} %reshape_reshape.3), calls=%async_computation.2 | async-start | bytes 1048576 | tf_op jit(solution)/shard_map/all_to_all | solution.py:22
  50.2 0.3 copy.27
  50.5 0.4 copy.26
  50.9 9.6 %all-to-all-done.2 = bf16[16,128,128]{2,1,0:T(8,128)(2,1)S(1)} async-done(((bf16[16,128,128]{2,1,0:T(8,128)(2,1)}), bf16[16,128,128]{2,1,0:T(8,128)(2,1)S(1)}, u32[]{:S(2)}, u32[]{:S(2)}) %all-to-all-start.2) | async-done | bytes 524320 | tf_op jit(solution)/shard_map/all_to_all | solution.py:22
  60.5 0.1 copy.23
  60.6 0.3 fusion.2
  61.0 0.1 copy.25
  61.1 8.0 %all-gather.2 = bf16[16,128,128]{2,1,0:T(8,128)(2,1)S(1)} all-gather(bf16[4,128,128]{2,1,0:T(8,128)(2,1)S(1)} %copy.25), channel_id=4, replica_groups=mesh['y'=4,'zq'=8,'zp'=2,'xl'=2,'xh'=2,'c'=2] {'xh','c'}, dimensions={0}, use_global_device_ids=true | all-gather | bytes 655360 | tf_op jit(solution)/shard_map/all_gather | solution.py:99
  69.2 0.5 fusion.10
  69.7 0.2 fusion.3
  69.9 0.2 convolution_convert_fusion.2
  70.2 0.3 fusion.27
  70.5 0.1 copy.40
  70.7 15.5 %all_to_all.31 = bf16[16,144,128]{2,1,0:T(8,128)(2,1)S(1)} all-to-all(bf16[16,144,128]{2,1,0:T(8,128)(2,1)S(1)} %maximum_bitcast_fusion), channel_id=1, replica_groups=mesh['y'=4,'zq'=8,'zp'=2,'xl'=2,'xh'=2,'c'=2] {'y','zp','xl'}, dimensions={0} | all-to-all | bytes 1179648 | tf_op jit(solution)/shard_map/all_to_all | solution.py:22
  86.3 0.2 fusion
  86.7 24.1 %all_to_all.32.parts_ref = bf16[8,144,128]{2,1,0:T(8,128)(2,1)S(1)} all-to-all(bf16[8,144,128]{2,1,0:T(8,128)(2,1)S(1)} %maximum_bitcast_fusion.1), channel_id=1, replica_groups={{64,80,96,112,0,16,32,48},{65,81,97,113,1,17,33,49},{66,82,98,114,2,18,..., dimensions={0} | all-to-all | bytes 589824 | tf_op jit(solution)/shard_map/all_to_all | solution.py:22
  110.8 0.7 sum_far.1
  111.4 3.5 %all-to-all-start.5 = ((bf16[16,24,128]{2,1,0:T(8,128)(2,1)}), bf16[16,24,128]{2,1,0:T(8,128)(2,1)S(1)}, u32[]{:S(2)}, u32[]{:S(2)}) async-start(bf16[16,24,128]{2,1,0:T(8,128)(2,1)} %sum_far.1), calls=%async_computation.5 | async-start | bytes 196608 | tf_op jit(solution)/shard_map/all_to_all | solution.py:22
  115.0 0.7 fusion.16
  115.6 6.6 %all-to-all-done.5.parts_ref = bf16[16,24,128]{2,1,0:T(8,128)(2,1)S(1)} async-done(((bf16[16,24,128]{2,1,0:T(8,128)(2,1)}), bf16[16,24,128]{2,1,0:T(8,128)(2,1)S(1)}, u32[]{:S(2)}, u32[]{:S(2)}) %all-to-all-start.5) | async-done | bytes 98336 | tf_op jit(solution)/shard_map/all_to_all | solution.py:22
  122.2 0.7 unpack.1
  (27 shorter events, 0.8 us)
Async XLA Ops:
  0.6 68.6 %copy-start = (bf16[128,256]{1,0:T(8,128)(2,1)S(1)}, bf16[128,256]{1,0:T(8,128)(2,1)}, u32[]{:S(2)}) copy-start(bf16[128,256]{1,0:T(8,128)(2,1)} %param.7) | copy-start | bytes 196612
  0.6 0.7 copy-start.2
  0.7 0.7 copy-start.3
  1.4 0.8 copy-start.1
  17.0 17.6 %copy-start.5 = (bf16[128,256]{1,0:T(8,128)(2,1)S(1)}, bf16[128,256]{1,0:T(8,128)(2,1)}, u32[]{:S(2)}) copy-start(bf16[128,256]{1,0:T(8,128)(2,1)} %param.8) | copy-start | bytes 196612
  17.0 28.0 %all-to-all-start.1 = ((bf16[8,128,128]{2,1,0:T(8,128)(2,1)}), bf16[8,128,128]{2,1,0:T(8,128)(2,1)S(1)}, u32[]{:S(2)}, u32[]{:S(2)}) async-start(bf16[8,128,128]{2,1,0:T(8,128)(2,1)} %broadcast_in_dim.18), calls=%async_computation.1 | async-start | bytes 524288 | tf_op jit(solution)/shard_map/all_to_all | solution.py:22
  46.5 3.7 %copy-start.4 = (bf16[4,1,4,128,128]{4,3,2,1,0:T(8,128)(2,1)S(1)}, bf16[4,1,4,128,128]{4,3,2,1,0:T(8,128)(2,1)}, u32[]{:S(2)}) copy-start(bf16[4,1,4,128,128]{4,3,2,1,0:T(8,128)(2,1)} %param.11) | copy-start | bytes 1572868
  46.5 14.0 %all-to-all-start.2 = ((bf16[16,128,128]{2,1,0:T(8,128)(2,1)}), bf16[16,128,128]{2,1,0:T(8,128)(2,1)S(1)}, u32[]{:S(2)}, u32[]{:S(2)}) async-start(bf16[16,128,128]{2,1,0:T(8,128)(2,1)} %reshape_reshape.3), calls=%async_computation.2 | async-start | bytes 1048576 | tf_op jit(solution)/shard_map/all_to_all | solution.py:22
  111.4 10.8 %all-to-all-start.5 = ((bf16[16,24,128]{2,1,0:T(8,128)(2,1)}), bf16[16,24,128]{2,1,0:T(8,128)(2,1)S(1)}, u32[]{:S(2)}, u32[]{:S(2)}) async-start(bf16[16,24,128]{2,1,0:T(8,128)(2,1)} %sum_far.1), calls=%async_computation.5 | async-start | bytes 196608 | tf_op jit(solution)/shard_map/all_to_all | solution.py:22

commit v7 on v6

--- a/solution.py
+++ b/solution.py
@@ -14,7 +14,17 @@
 CUT = TILE // NM
 
 
-ORDER = [(index + NQ // 2) % NQ for index in range(NQ)]
+AHEAD, BACK = 5, 4
+
+
+def order(lead):
+    return [[(index + lead) % NQ for index in range(NQ)]]
+
+
+def rows_in(lead):
+    place = jnp.arange(NQ * NM, dtype=jnp.int32)
+    zq = (place // NM + lead) % NQ
+    return ((place // (NZP * NX)) % NY) * (NQ * NZP * NX) + zq * (NZP * NX) + place % (NZP * NX)
 
 
 def exchange(array, axes, groups=None):
@@ -82,17 +92,16 @@
     )(features, tile_owners.reshape(blocks, slots), tile_counts.reshape(1, blocks))
     first = exchange(start, NEAR)
     spread = jnp.broadcast_to(first[None, :, :CUT], (NQ, NM, CUT, width)).reshape(NQ, NM * CUT, width)
-    table = exchange(spread, "zq", [ORDER])
+    table = exchange(spread, "zq", order(AHEAD))
     codes = first[:, CUT, :total].astype(jnp.int32).reshape(NM * total)
-    place = jnp.arange(NQ * NM, dtype=jnp.int32)
-    ident = ((place // (NZP * NX)) % NY) * (NQ * NZP * NX) + ((place // NM + NQ // 2) % NQ) * (NZP * NX) + place % (NZP * NX)
-    pick = (codes[:, None] == ident[None, :]).astype(bf16)
+    choose = (codes[:, None] == rows_in(AHEAD)[None, :]).astype(bf16)
+    pick = (codes[:, None] == rows_in(BACK)[None, :]).astype(bf16)
     halves = jnp.stack([upstream[:, :width], upstream[:, width:]])
     first, halves = lax.optimization_barrier((first, halves))
     upstream_all = lax.all_gather(lax.all_gather(halves, "xh", axis=0), "c", axis=1)
-    table, upstream_all, pick = lax.optimization_barrier((table, upstream_all, pick))
+    table, upstream_all, choose, pick = lax.optimization_barrier((table, upstream_all, choose, pick))
     table = table.reshape(NQ * NM, CUT * width)
-    wanted = jnp.dot(pick, table, preferred_element_type=f32).astype(bf16)
+    wanted = jnp.dot(choose, table, preferred_element_type=f32).astype(bf16)
     third = exchange(wanted.reshape(NM, total, CUT, width), NEAR)
     picked = third.transpose(1, 0, 2, 3).reshape(blocks, slots, TILE, width)
     partial_value = jnp.einsum("btij,btjf->bif", values, picked, preferred_element_type=f32).astype(bf16)
@@ -122,7 +131,7 @@
             axis=1,
         ).reshape(NQ, (NM + 2) * CUT, width),
         "zq",
-        [ORDER],
+        order(BACK),
     )
     packed = pl.pallas_call(
         sum_kernel,

time: 124 us -> 122 us (0.984)
  starting transfers between devices: 24.8 us -> 23 us
    all_to_all x3, starting transfers between devices: 24.8 us -> 23 us  [exchange(): lax.all_to_all(flat, axes, split_axis=0, concat_axis=0, axis_index_groups...]
where the time goes in v7:
time: 122 us
  blocking collectives  69.9 us (57%)
  starting transfers between devices  23 us (19%)
  waiting for transfers between devices  18.3 us (15%)
  local copies, waits for them, and re-layouts  4.61 us (4%)
  matrix products  2.09 us (2%)
  Pallas kernels  1.96 us (2%)
    all_to_all x3, blocking collectives, exchange(): lax.all_to_all(flat, axes, split_axis=0, concat_axis=0, axis_index_groups...  53.5 us
    all_to_all x3, starting transfers between devices, exchange(): lax.all_to_all(flat, axes, split_axis=0, concat_axis=0, axis_index_groups...  23 us
    all_to_all x3, waiting for transfers between devices, exchange(): lax.all_to_all(flat, axes, split_axis=0, concat_axis=0, axis_index_groups...  18.3 us
    all_gather x1, blocking collectives, body(): shared = lax.all_gather(partial_value, REP, axis=0)  8.02 us
    all_gather x1, blocking collectives, body(): lax.all_gather(halves, 'xh', axis=0)  6.44 us
  transfers between devices with their start and end apart: 3, of which 3 were waited for; matrix products, arithmetic and copies ran while one was open for 1% of the time, Pallas kernels for 0%

profile of v7, /device:TPU:4, one launch (start us, length us, event | category | flops | bytes accessed | tf_op | source)
XLA Modules:
  0.0 121.8 jit_solution(12806046901845706326)
XLA Ops:
  0.7 0.7 copy-done.2
  1.4 0.8 copy-done.1
  2.1 0.6 start.1
  2.7 13.6 %all_to_all.30 = bf16[16,16,128]{2,1,0:T(8,128)(2,1)S(1)} all-to-all(bf16[16,16,128]{2,1,0:T(8,128)(2,1)S(1)} %start.1), channel_id=1, replica_groups=mesh['y'=4,'zq'=8,'zp'=2,'xl'=2,'xh'=2,'c'=2] {'y','zp','xl'}, dimensions={0} | all-to-all | bytes 131072 | tf_op jit(solution)/shard_map/all_to_all | solution.py:32
  16.3 0.7 broadcast_in_dim.9
  17.0 15.8 %all-to-all-start.1 = ((bf16[8,128,128]{2,1,0:T(8,128)(2,1)}), bf16[8,128,128]{2,1,0:T(8,128)(2,1)S(1)}, u32[]{:S(2)}, u32[]{:S(2)}) async-start(bf16[8,128,128]{2,1,0:T(8,128)(2,1)} %broadcast_in_dim.9), calls=%async_computation.1 | async-start | bytes 524288 | tf_op jit(solution)/shard_map/all_to_all | solution.py:32
  33.0 6.4 %all-gather = bf16[4,128,128]{2,1,0:T(8,128)(2,1)S(1)} all-gather(bf16[2,128,128]{2,1,0:T(8,128)(2,1)S(1)} %pad_maximum_fusion), channel_id=2, replica_groups=mesh['y'=4,'zq'=8,'zp'=2,'xl'=2,'xh'=2,'c'=2] {'xh'}, dimensions={0}, use_global_device_ids=true | all-gather | bytes 196608 | tf_op jit(solution)/shard_map/all_gather | solution.py:101
  39.4 2.0 %all-gather.1 = bf16[2,4,128,128]{3,2,1,0:T(8,128)(2,1)S(1)} all-gather(bf16[2,2,128,128]{3,2,1,0:T(8,128)(2,1)S(1)} %bitcast.103), channel_id=3, replica_groups=mesh['y'=4,'zq'=8,'zp'=2,'xl'=2,'xh'=2,'c'=2] {'c'}, dimensions={1}, use_global_device_ids=true | all-gather | bytes 393216 | tf_op jit(solution)/shard_map/all_gather | solution.py:101
  41.5 3.5 %all-to-all-done.1 = bf16[8,128,128]{2,1,0:T(8,128)(2,1)S(1)} async-done(((bf16[8,128,128]{2,1,0:T(8,128)(2,1)}), bf16[8,128,128]{2,1,0:T(8,128)(2,1)S(1)}, u32[]{:S(2)}, u32[]{:S(2)}) %all-to-all-start.1) | async-done | bytes 262176 | tf_op jit(solution)/shard_map/all_to_all | solution.py:32
  45.2 0.3 convolution_convert_fusion
  45.5 1.0 reshape_reshape.3
  46.5 3.7 %all-to-all-start.2 = ((bf16[16,128,128]{2,1,0:T(8,128)(2,1)}), bf16[16,128,128]{2,1,0:T(8,128)(2,1)S(1)}, u32[]{:S(2)}, u32[]{:S(2)}) async-start(bf16[16,128,128]{2,1,0:T(8,128)(2,1)} %reshape_reshape.3), calls=%async_computation.2 | async-start | bytes 1048576 | tf_op jit(solution)/shard_map/all_to_all | solution.py:32
  50.2 0.3 copy.27
  50.5 0.4 copy.26
  50.9 8.1 %all-to-all-done.2 = bf16[16,128,128]{2,1,0:T(8,128)(2,1)S(1)} async-done(((bf16[16,128,128]{2,1,0:T(8,128)(2,1)}), bf16[16,128,128]{2,1,0:T(8,128)(2,1)S(1)}, u32[]{:S(2)}, u32[]{:S(2)}) %all-to-all-start.2) | async-done | bytes 524320 | tf_op jit(solution)/shard_map/all_to_all | solution.py:32
  59.1 0.1 copy.23
  59.2 0.3 fusion.2
  59.6 0.1 copy.25
  59.7 8.0 %all-gather.2 = bf16[16,128,128]{2,1,0:T(8,128)(2,1)S(1)} all-gather(bf16[4,128,128]{2,1,0:T(8,128)(2,1)S(1)} %copy.25), channel_id=4, replica_groups=mesh['y'=4,'zq'=8,'zp'=2,'xl'=2,'xh'=2,'c'=2] {'xh','c'}, dimensions={0}, use_global_device_ids=true | all-gather | bytes 655360 | tf_op jit(solution)/shard_map/all_gather | solution.py:108
  67.8 0.5 fusion.10
  68.3 0.2 fusion.3
  68.5 0.2 convolution_convert_fusion.2
  68.8 0.3 fusion.30
  69.2 0.1 copy.40
  69.4 15.5 %all_to_all.31 = bf16[16,144,128]{2,1,0:T(8,128)(2,1)S(1)} all-to-all(bf16[16,144,128]{2,1,0:T(8,128)(2,1)S(1)} %maximum_bitcast_fusion), channel_id=1, replica_groups=mesh['y'=4,'zq'=8,'zp'=2,'xl'=2,'xh'=2,'c'=2] {'y','zp','xl'}, dimensions={0} | all-to-all | bytes 1179648 | tf_op jit(solution)/shard_map/all_to_all | solution.py:32
  84.9 0.2 fusion
  85.3 24.4 %all_to_all.32.parts_ref = bf16[8,144,128]{2,1,0:T(8,128)(2,1)S(1)} all-to-all(bf16[8,144,128]{2,1,0:T(8,128)(2,1)S(1)} %maximum_bitcast_fusion.1), channel_id=1, replica_groups={{64,80,96,112,0,16,32,48},{65,81,97,113,1,17,33,49},{66,82,98,114,2,18,..., dimensions={0} | all-to-all | bytes 589824 | tf_op jit(solution)/shard_map/all_to_all | solution.py:32
  109.7 0.7 sum_far.1
  110.4 3.5 %all-to-all-start.5 = ((bf16[16,24,128]{2,1,0:T(8,128)(2,1)}), bf16[16,24,128]{2,1,0:T(8,128)(2,1)S(1)}, u32[]{:S(2)}, u32[]{:S(2)}) async-start(bf16[16,24,128]{2,1,0:T(8,128)(2,1)} %sum_far.1), calls=%async_computation.5 | async-start | bytes 196608 | tf_op jit(solution)/shard_map/all_to_all | solution.py:32
  113.9 0.7 fusion.16
  114.6 6.6 %all-to-all-done.5.parts_ref = bf16[16,24,128]{2,1,0:T(8,128)(2,1)S(1)} async-done(((bf16[16,24,128]{2,1,0:T(8,128)(2,1)}), bf16[16,24,128]{2,1,0:T(8,128)(2,1)S(1)}, u32[]{:S(2)}, u32[]{:S(2)}) %all-to-all-start.5) | async-done | bytes 98336 | tf_op jit(solution)/shard_map/all_to_all | solution.py:32
  121.1 0.7 unpack.1
  (27 shorter events, 0.8 us)
Async XLA Ops:
  0.6 67.2 %copy-start = (bf16[128,256]{1,0:T(8,128)(2,1)S(1)}, bf16[128,256]{1,0:T(8,128)(2,1)}, u32[]{:S(2)}) copy-start(bf16[128,256]{1,0:T(8,128)(2,1)} %param.7) | copy-start | bytes 196612
  0.6 0.7 copy-start.2
  0.7 0.7 copy-start.3
  1.4 0.8 copy-start.1
  17.0 15.8 %copy-start.5 = (bf16[128,256]{1,0:T(8,128)(2,1)S(1)}, bf16[128,256]{1,0:T(8,128)(2,1)}, u32[]{:S(2)}) copy-start(bf16[128,256]{1,0:T(8,128)(2,1)} %param.8) | copy-start | bytes 196612
  17.0 28.0 %all-to-all-start.1 = ((bf16[8,128,128]{2,1,0:T(8,128)(2,1)}), bf16[8,128,128]{2,1,0:T(8,128)(2,1)S(1)}, u32[]{:S(2)}, u32[]{:S(2)}) async-start(bf16[8,128,128]{2,1,0:T(8,128)(2,1)} %broadcast_in_dim.9), calls=%async_computation.1 | async-start | bytes 524288 | tf_op jit(solution)/shard_map/all_to_all | solution.py:32
  46.5 3.7 %copy-start.4 = (bf16[4,1,4,128,128]{4,3,2,1,0:T(8,128)(2,1)S(1)}, bf16[4,1,4,128,128]{4,3,2,1,0:T(8,128)(2,1)}, u32[]{:S(2)}) copy-start(bf16[4,1,4,128,128]{4,3,2,1,0:T(8,128)(2,1)} %param.11) | copy-start | bytes 1572868
  46.5 12.6 %all-to-all-start.2 = ((bf16[16,128,128]{2,1,0:T(8,128)(2,1)}), bf16[16,128,128]{2,1,0:T(8,128)(2,1)S(1)}, u32[]{:S(2)}, u32[]{:S(2)}) async-start(bf16[16,128,128]{2,1,0:T(8,128)(2,1)} %reshape_reshape.3), calls=%async_computation.2 | async-start | bytes 1048576 | tf_op jit(solution)/shard_map/all_to_all | solution.py:32
  110.4 10.8 %all-to-all-start.5 = ((bf16[16,24,128]{2,1,0:T(8,128)(2,1)}), bf16[16,24,128]{2,1,0:T(8,128)(2,1)S(1)}, u32[]{:S(2)}, u32[]{:S(2)}) async-start(bf16[16,24,128]{2,1,0:T(8,128)(2,1)} %sum_far.1), calls=%async_computation.5 | async-start | bytes 196608 | tf_op jit(solution)/shard_map/all_to_all | solution.py:32

commit v8 on v7

--- a/solution.py
+++ b/solution.py
@@ -21,6 +21,10 @@
     return [[(index + lead) % NQ for index in range(NQ)]]
 
 
+def swap(array):
+    return jnp.concatenate([array[NM // 2 :], array[: NM // 2]])
+
+
 def rows_in(lead):
     place = jnp.arange(NQ * NM, dtype=jnp.int32)
     zq = (place // NM + lead) % NQ
@@ -40,7 +44,16 @@
     return total
 
 
-def start_kernel(features_ref, owners_ref, counts_ref, out_ref):
+def start_kernel(features_in, owners_in, counts_in, out_ref, features_ref, owners_ref, counts_ref, done):
+    copies = [
+        pltpu.make_async_copy(owners_in, owners_ref, done.at[0]),
+        pltpu.make_async_copy(counts_in, counts_ref, done.at[1]),
+        pltpu.make_async_copy(features_in, features_ref, done.at[2]),
+    ]
+    for copy in copies:
+        copy.start()
+    for copy in copies:
+        copy.wait()
     width = features_ref.shape[1]
     blocks, slots = owners_ref.shape
     lane = lax.broadcasted_iota(jnp.int32, (CUT, width), 1)
@@ -50,7 +63,7 @@
             wanted = jnp.where(slot < counts_ref[0, block], owners_ref[block, slot], -1)
             code = jnp.where(lane == block * slots + slot, wanted, code)
     code = jnp.broadcast_to(code.astype(jnp.float32)[None], (NM, CUT, width))
-    cut = features_ref[...].astype(jnp.float32).reshape(NM, CUT, width)
+    cut = swap(features_ref[...].astype(jnp.float32).reshape(NM, CUT, width))
     out_ref[...] = jnp.concatenate([cut, code], axis=1).astype(out_ref.dtype)
 
 
@@ -85,12 +98,16 @@
     start = pl.pallas_call(
         start_kernel,
         out_shape=jax.ShapeDtypeStruct((NM, 2 * CUT, width), bf16),
-        in_specs=[near, scalar, scalar],
-        out_specs=near,
-        compiler_params=room,
+        in_specs=[pl.BlockSpec(memory_space=pl.ANY)] * 3,
+        scratch_shapes=[
+            pltpu.VMEM((TILE, width), bf16),
+            pltpu.SMEM((blocks, slots), jnp.int32),
+            pltpu.SMEM((1, blocks), jnp.int32),
+            pltpu.SemaphoreType.DMA((3,)),
+        ],
         name="start",
     )(features, tile_owners.reshape(blocks, slots), tile_counts.reshape(1, blocks))
-    first = exchange(start, NEAR)
+    first = swap(exchange(start, NEAR, [[index ^ (NM // 2) for index in range(NM)]]))
     spread = jnp.broadcast_to(first[None, :, :CUT], (NQ, NM, CUT, width)).reshape(NQ, NM * CUT, width)
     table = exchange(spread, "zq", order(AHEAD))
     codes = first[:, CUT, :total].astype(jnp.int32).reshape(NM * total)

time: 122 us -> 121 us (level)
  local copies, waits for them, and re-layouts: 4.61 us -> 3.16 us
  blocking collectives: 69.9 us -> 68.5 us
    unnamed x13 -> x7, local copies, waits for them, and re-layouts: 1.52 us -> 0.06 us
    all_to_all x3, blocking collectives: 53.5 us -> 52.1 us  [exchange(): lax.all_to_all(flat, axes, split_axis=0, concat_axis=0, axis_index_groups...]
where the time goes in v8:
time: 121 us
  blocking collectives  68.5 us (57%)
  starting transfers between devices  23.6 us (20%)
  waiting for transfers between devices  18.4 us (15%)
  local copies, waits for them, and re-layouts  3.16 us (3%)
  Pallas kernels  2.88 us (2%)
  matrix products  2.09 us (2%)
    all_to_all x3, blocking collectives, exchange(): lax.all_to_all(flat, axes, split_axis=0, concat_axis=0, axis_index_groups...  52.1 us
    all_to_all x3, starting transfers between devices, exchange(): lax.all_to_all(flat, axes, split_axis=0, concat_axis=0, axis_index_groups...  23.6 us
    all_to_all x3, waiting for transfers between devices, exchange(): lax.all_to_all(flat, axes, split_axis=0, concat_axis=0, axis_index_groups...  18.4 us
    all_gather x1, blocking collectives, body(): shared = lax.all_gather(partial_value, REP, axis=0)  8.02 us
    all_gather x1, blocking collectives, body(): lax.all_gather(halves, 'xh', axis=0)  6.45 us
  transfers between devices with their start and end apart: 3, of which 3 were waited for; matrix products, arithmetic and copies ran while one was open for 1% of the time, Pallas kernels for 0%

profile of v8, /device:TPU:4, one launch (start us, length us, event | category | flops | bytes accessed | tf_op | source)
XLA Modules:
  0.0 120.6 jit_solution(8103421152294571566)
XLA Ops:
  0.6 1.5 %start.1 = bf16[16,16,128]{2,1,0:T(8,128)(2,1)} custom-call(bf16[128,128]{1,0:T(8,128)(2,1)} %features_in.1, s32[4,4]{1,0:T(4,128)} %bitcast.104, s32[1,4]{1,0:T(1,128)} %bitcast.105), custom_call_target="tpu_custom_call" | custom-call | tf_op jit(solution)/shard_map/start/pallas_call | solution.py:98
  2.2 12.2 %all_to_all.30 = bf16[16,16,128]{2,1,0:T(8,128)(2,1)S(1)} all-to-all(bf16[16,16,128]{2,1,0:T(8,128)(2,1)} %start.1), channel_id=1, replica_groups={{256,260,264,268,384,388,392,396,0,4,8,12,128,132,136,140},{257,261,265..., dimensions={0} | all-to-all | bytes 131072 | tf_op jit(solution)/shard_map/all_to_all | solution.py:36
  14.3 0.7 broadcast_in_dim.9
  15.1 15.8 %all-to-all-start.1 = ((bf16[8,128,128]{2,1,0:T(8,128)(2,1)}), bf16[8,128,128]{2,1,0:T(8,128)(2,1)S(1)}, u32[]{:S(2)}, u32[]{:S(2)}) async-start(bf16[8,128,128]{2,1,0:T(8,128)(2,1)} %broadcast_in_dim.9), calls=%async_computation.1 | async-start | bytes 524288 | tf_op jit(solution)/shard_map/all_to_all | solution.py:36
  30.9 6.4 %all-gather = bf16[4,128,128]{2,1,0:T(8,128)(2,1)S(1)} all-gather(bf16[2,128,128]{2,1,0:T(8,128)(2,1)S(1)} %pad_maximum_fusion.1), channel_id=2, replica_groups=mesh['y'=4,'zq'=8,'zp'=2,'xl'=2,'xh'=2,'c'=2] {'xh'}, dimensions={0}, use_global_device_ids=true | all-gather | bytes 196608 | tf_op jit(solution)/shard_map/all_gather | solution.py:118
  37.4 2.0 %all-gather.1 = bf16[2,4,128,128]{3,2,1,0:T(8,128)(2,1)S(1)} all-gather(bf16[2,2,128,128]{3,2,1,0:T(8,128)(2,1)S(1)} %bitcast.101), channel_id=3, replica_groups=mesh['y'=4,'zq'=8,'zp'=2,'xl'=2,'xh'=2,'c'=2] {'c'}, dimensions={1}, use_global_device_ids=true | all-gather | bytes 393216 | tf_op jit(solution)/shard_map/all_gather | solution.py:118
  39.5 0.1 compare_convert_fusion
  39.6 3.6 %all-to-all-done.1 = bf16[8,128,128]{2,1,0:T(8,128)(2,1)S(1)} async-done(((bf16[8,128,128]{2,1,0:T(8,128)(2,1)}), bf16[8,128,128]{2,1,0:T(8,128)(2,1)S(1)}, u32[]{:S(2)}, u32[]{:S(2)}) %all-to-all-start.1) | async-done | bytes 262176 | tf_op jit(solution)/shard_map/all_to_all | solution.py:36
  43.2 0.1 reshape.146
  43.4 0.3 convolution_convert_fusion
  43.6 1.0 reshape_reshape.3
  44.7 4.3 %all-to-all-start.2 = ((bf16[16,128,128]{2,1,0:T(8,128)(2,1)}), bf16[16,128,128]{2,1,0:T(8,128)(2,1)S(1)}, u32[]{:S(2)}, u32[]{:S(2)}) async-start(bf16[16,128,128]{2,1,0:T(8,128)(2,1)} %reshape_reshape.3), calls=%async_computation.2 | async-start | bytes 1048576 | tf_op jit(solution)/shard_map/all_to_all | solution.py:36
  49.0 0.3 copy.27
  49.3 0.4 copy.26
  49.7 8.2 %all-to-all-done.2 = bf16[16,128,128]{2,1,0:T(8,128)(2,1)S(1)} async-done(((bf16[16,128,128]{2,1,0:T(8,128)(2,1)}), bf16[16,128,128]{2,1,0:T(8,128)(2,1)S(1)}, u32[]{:S(2)}, u32[]{:S(2)}) %all-to-all-start.2) | async-done | bytes 524320 | tf_op jit(solution)/shard_map/all_to_all | solution.py:36
  57.9 0.1 copy.23
  58.0 0.3 fusion.2
  58.4 0.1 copy.25
  58.5 8.0 %all-gather.2 = bf16[16,128,128]{2,1,0:T(8,128)(2,1)S(1)} all-gather(bf16[4,128,128]{2,1,0:T(8,128)(2,1)S(1)} %copy.25), channel_id=4, replica_groups=mesh['y'=4,'zq'=8,'zp'=2,'xl'=2,'xh'=2,'c'=2] {'xh','c'}, dimensions={0}, use_global_device_ids=true | all-gather | bytes 655360 | tf_op jit(solution)/shard_map/all_gather | solution.py:125
  66.6 0.5 fusion.10
  67.1 0.2 fusion.3
  67.3 0.2 convolution_convert_fusion.2
  67.6 0.3 fusion.33
  67.9 0.1 copy.40
  68.2 15.5 %all_to_all.31 = bf16[16,144,128]{2,1,0:T(8,128)(2,1)S(1)} all-to-all(bf16[16,144,128]{2,1,0:T(8,128)(2,1)S(1)} %maximum_bitcast_fusion), channel_id=1, replica_groups=mesh['y'=4,'zq'=8,'zp'=2,'xl'=2,'xh'=2,'c'=2] {'y','zp','xl'}, dimensions={0} | all-to-all | bytes 1179648 | tf_op jit(solution)/shard_map/all_to_all | solution.py:36
  83.7 0.2 fusion
  84.1 24.4 %all_to_all.32.parts_ref = bf16[8,144,128]{2,1,0:T(8,128)(2,1)S(1)} all-to-all(bf16[8,144,128]{2,1,0:T(8,128)(2,1)S(1)} %maximum_bitcast_fusion.1), channel_id=1, replica_groups={{64,80,96,112,0,16,32,48},{65,81,97,113,1,17,33,49},{66,82,98,114,2,18,..., dimensions={0} | all-to-all | bytes 589824 | tf_op jit(solution)/shard_map/all_to_all | solution.py:36
  108.5 0.7 sum_far.1
  109.2 3.5 %all-to-all-start.5 = ((bf16[16,24,128]{2,1,0:T(8,128)(2,1)}), bf16[16,24,128]{2,1,0:T(8,128)(2,1)S(1)}, u32[]{:S(2)}, u32[]{:S(2)}) async-start(bf16[16,24,128]{2,1,0:T(8,128)(2,1)} %sum_far.1), calls=%async_computation.5 | async-start | bytes 196608 | tf_op jit(solution)/shard_map/all_to_all | solution.py:36
  112.7 0.7 fusion.16
  113.4 6.6 %all-to-all-done.5.parts_ref = bf16[16,24,128]{2,1,0:T(8,128)(2,1)S(1)} async-done(((bf16[16,24,128]{2,1,0:T(8,128)(2,1)}), bf16[16,24,128]{2,1,0:T(8,128)(2,1)S(1)}, u32[]{:S(2)}, u32[]{:S(2)}) %all-to-all-start.5) | async-done | bytes 98336 | tf_op jit(solution)/shard_map/all_to_all | solution.py:36
  119.9 0.7 unpack.1
  (22 shorter events, 0.6 us)
Async XLA Ops:
  0.6 66.0 %copy-start = (bf16[128,256]{1,0:T(8,128)(2,1)S(1)}, bf16[128,256]{1,0:T(8,128)(2,1)}, u32[]{:S(2)}) copy-start(bf16[128,256]{1,0:T(8,128)(2,1)} %param.7) | copy-start | bytes 196612
  15.1 15.8 %copy-start.2 = (bf16[128,256]{1,0:T(8,128)(2,1)S(1)}, bf16[128,256]{1,0:T(8,128)(2,1)}, u32[]{:S(2)}) copy-start(bf16[128,256]{1,0:T(8,128)(2,1)} %param.8) | copy-start | bytes 196612
  15.1 28.1 %all-to-all-start.1 = ((bf16[8,128,128]{2,1,0:T(8,128)(2,1)}), bf16[8,128,128]{2,1,0:T(8,128)(2,1)S(1)}, u32[]{:S(2)}, u32[]{:S(2)}) async-start(bf16[8,128,128]{2,1,0:T(8,128)(2,1)} %broadcast_in_dim.9), calls=%async_computation.1 | async-start | bytes 524288 | tf_op jit(solution)/shard_map/all_to_all | solution.py:36
  44.7 4.3 %copy-start.1 = (bf16[4,1,4,128,128]{4,3,2,1,0:T(8,128)(2,1)S(1)}, bf16[4,1,4,128,128]{4,3,2,1,0:T(8,128)(2,1)}, u32[]{:S(2)}) copy-start(bf16[4,1,4,128,128]{4,3,2,1,0:T(8,128)(2,1)} %param.11) | copy-start | bytes 1572868
  44.7 13.2 %all-to-all-start.2 = ((bf16[16,128,128]{2,1,0:T(8,128)(2,1)}), bf16[16,128,128]{2,1,0:T(8,128)(2,1)S(1)}, u32[]{:S(2)}, u32[]{:S(2)}) async-start(bf16[16,128,128]{2,1,0:T(8,128)(2,1)} %reshape_reshape.3), calls=%async_computation.2 | async-start | bytes 1048576 | tf_op jit(solution)/shard_map/all_to_all | solution.py:36
  109.2 10.8 %all-to-all-start.5 = ((bf16[16,24,128]{2,1,0:T(8,128)(2,1)}), bf16[16,24,128]{2,1,0:T(8,128)(2,1)S(1)}, u32[]{:S(2)}, u32[]{:S(2)}) async-start(bf16[16,24,128]{2,1,0:T(8,128)(2,1)} %sum_far.1), calls=%async_computation.5 | async-start | bytes 196608 | tf_op jit(solution)/shard_map/all_to_all | solution.py:36

commit v9 on v8

--- a/solution.py
+++ b/solution.py
@@ -67,6 +67,10 @@
     out_ref[...] = jnp.concatenate([cut, code], axis=1).astype(out_ref.dtype)
 
 
+def keep_kernel(weight_ref, out_ref):
+    out_ref[...] = weight_ref[...]
+
+
 def sum_kernel(parts_ref, out_ref):
     sums = parts_ref[0].astype(jnp.float32)
     for index in range(1, NQ):
@@ -114,9 +118,21 @@
     choose = (codes[:, None] == rows_in(AHEAD)[None, :]).astype(bf16)
     pick = (codes[:, None] == rows_in(BACK)[None, :]).astype(bf16)
     halves = jnp.stack([upstream[:, :width], upstream[:, width:]])
-    first, halves = lax.optimization_barrier((first, halves))
+    first, halves, weight = lax.optimization_barrier((first, halves, weight))
     upstream_all = lax.all_gather(lax.all_gather(halves, "xh", axis=0), "c", axis=1)
-    table, upstream_all, choose, pick = lax.optimization_barrier((table, upstream_all, choose, pick))
+    upstream_all = upstream_all.transpose(0, 1, 3, 2, 4).reshape(blocks * TILE, 2 * width).astype(f32)
+    turned = jnp.swapaxes(values, 2, 3)
+    weight = pl.pallas_call(
+        keep_kernel,
+        out_shape=jax.ShapeDtypeStruct(weight.shape, bf16),
+        in_specs=[near],
+        out_specs=near,
+        compiler_params=room,
+        name="keep",
+    )(weight)
+    table, upstream_all, turned, weight, choose, pick = lax.optimization_barrier(
+        (table, upstream_all, turned, weight, choose, pick)
+    )
     table = table.reshape(NQ * NM, CUT * width)
     wanted = jnp.dot(choose, table, preferred_element_type=f32).astype(bf16)
     third = exchange(wanted.reshape(NM, total, CUT, width), NEAR)
@@ -124,15 +140,14 @@
     partial_value = jnp.einsum("btij,btjf->bif", values, picked, preferred_element_type=f32).astype(bf16)
     shared = lax.all_gather(partial_value, REP, axis=0)
     aggregated = add_up(shared).astype(bf16).reshape(blocks * TILE, width)
-    upstream_all = upstream_all.transpose(0, 1, 3, 2, 4).reshape(blocks * TILE, 2 * width)
 
     pre_act = jnp.dot(aggregated, weight, preferred_element_type=f32)
     hidden_all, pullback = jax.vjp(jax.nn.gelu, pre_act)
     hidden = lax.dynamic_slice_in_dim(hidden_all.astype(bf16), lax.axis_index(REP) * TILE, TILE, 0)
-    slope = pullback(upstream_all.astype(f32))[0].astype(bf16)
+    slope = pullback(upstream_all)[0].astype(bf16)
     weight_part = jnp.dot(aggregated.T, slope, preferred_element_type=f32)
     back_rows = jnp.dot(slope, weight.T, preferred_element_type=f32).astype(bf16).reshape(blocks, TILE, width)
-    parts = jnp.einsum("btji,bjf->btif", values, back_rows, preferred_element_type=f32).astype(bf16)
+    parts = jnp.einsum("btij,bjf->btif", turned, back_rows, preferred_element_type=f32).astype(bf16)
 
     parts = parts.reshape(total, NM, CUT, width).transpose(1, 0, 2, 3)
     weight_cut = weight_part.astype(bf16).reshape(NM, CUT, 2, width).transpose(0, 2, 1, 3)

time: 121 us -> 120 us (level)
  blocking collectives: 68.5 us -> 81.4 us
  waiting for transfers between devices: 18.4 us -> 8.92 us
  starting transfers between devices: 23.6 us -> 19.3 us
    all_to_all x3 -> x4, blocking collectives: 52.1 us -> 65 us  [exchange(): lax.all_to_all(flat, axes, split_axis=0, concat_axis=0, axis_index_groups...]
    all_to_all x3 -> x2, waiting for transfers between devices: 18.4 us -> 8.92 us  [exchange(): lax.all_to_all(flat, axes, split_axis=0, concat_axis=0, axis_index_groups...]
    all_to_all x3 -> x2, starting transfers between devices: 23.6 us -> 19.3 us  [exchange(): lax.all_to_all(flat, axes, split_axis=0, concat_axis=0, axis_index_groups...]
  transfers between devices with their start and end apart: 3 -> 2, of which waited for: 3 -> 2; matrix products, arithmetic and copies ran while one was open for 1% -> 1% of each run, Pallas kernels for 0% -> 0%
where the time goes in v9:
time: 120 us; the launch traced here: 119 us
  blocking collectives  81.4 us (68%)
  starting transfers between devices  19.3 us (16%)
  waiting for transfers between devices  8.92 us (7%)
  local copies, waits for them, and re-layouts  2.9 us (2%)
  Pallas kernels  2.88 us (2%)
  matrix products  2.16 us (2%)
    all_to_all x4, blocking collectives, exchange(): lax.all_to_all(flat, axes, split_axis=0, concat_axis=0, axis_index_groups...  65 us
    all_to_all x2, starting transfers between devices, exchange(): lax.all_to_all(flat, axes, split_axis=0, concat_axis=0, axis_index_groups...  19.3 us
    all_to_all x2, waiting for transfers between devices, exchange(): lax.all_to_all(flat, axes, split_axis=0, concat_axis=0, axis_index_groups...  8.92 us
    all_gather x1, blocking collectives, body(): shared = lax.all_gather(partial_value, REP, axis=0)  8.02 us
    all_gather x1, blocking collectives, body(): lax.all_gather(halves, 'xh', axis=0)  6.45 us
  transfers between devices with their start and end apart: 2, of which 2 were waited for; matrix products, arithmetic and copies ran while one was open for 1% of the time, Pallas kernels for 0%

profile of v9, /device:TPU:4, one launch (start us, length us, event | category | flops | bytes accessed | tf_op | source)
XLA Modules:
  0.0 119.5 jit_solution(10808306948502415418)
XLA Ops:
  0.6 1.5 %start.1 = bf16[16,16,128]{2,1,0:T(8,128)(2,1)} custom-call(bf16[128,128]{1,0:T(8,128)(2,1)} %features_in.1, s32[4,4]{1,0:T(4,128)} %bitcast.94, s32[1,4]{1,0:T(1,128)} %bitcast.95), custom_call_target="tpu_custom_call" | custom-call | tf_op jit(solution)/shard_map/start/pallas_call | solution.py:102
  2.2 12.2 %all_to_all.30 = bf16[16,16,128]{2,1,0:T(8,128)(2,1)S(1)} all-to-all(bf16[16,16,128]{2,1,0:T(8,128)(2,1)} %start.1), channel_id=1, replica_groups={{256,260,264,268,384,388,392,396,0,4,8,12,128,132,136,140},{257,261,265..., dimensions={0} | all-to-all | bytes 131072 | tf_op jit(solution)/shard_map/all_to_all | solution.py:36
  14.3 0.7 broadcast_in_dim.9
  15.1 15.8 %all-to-all-start.1 = ((bf16[8,128,128]{2,1,0:T(8,128)(2,1)}), bf16[8,128,128]{2,1,0:T(8,128)(2,1)S(1)}, u32[]{:S(2)}, u32[]{:S(2)}) async-start(bf16[8,128,128]{2,1,0:T(8,128)(2,1)} %broadcast_in_dim.9), calls=%async_computation.1 | async-start | bytes 524288 | tf_op jit(solution)/shard_map/all_to_all | solution.py:36
  30.9 6.4 %all-gather = bf16[4,128,128]{2,1,0:T(8,128)(2,1)S(1)} all-gather(bf16[2,128,128]{2,1,0:T(8,128)(2,1)S(1)} %pad_maximum_fusion.1), channel_id=2, replica_groups=mesh['y'=4,'zq'=8,'zp'=2,'xl'=2,'xh'=2,'c'=2] {'xh'}, dimensions={0}, use_global_device_ids=true | all-gather | bytes 196608 | tf_op jit(solution)/shard_map/all_gather | solution.py:122
  37.4 2.0 %all-gather.1 = bf16[2,4,128,128]{3,2,1,0:T(8,128)(2,1)S(1)} all-gather(bf16[2,2,128,128]{3,2,1,0:T(8,128)(2,1)S(1)} %bitcast.92), channel_id=3, replica_groups=mesh['y'=4,'zq'=8,'zp'=2,'xl'=2,'xh'=2,'c'=2] {'c'}, dimensions={1}, use_global_device_ids=true | all-gather | bytes 393216 | tf_op jit(solution)/shard_map/all_gather | solution.py:122
  39.4 0.4 copy.23
  39.9 0.8 copy-done.1
  40.7 0.1 reshape.158
  40.8 0.1 compare_convert_fusion
  40.9 2.3 %all-to-all-done.1 = bf16[8,128,128]{2,1,0:T(8,128)(2,1)S(1)} async-done(((bf16[8,128,128]{2,1,0:T(8,128)(2,1)}), bf16[8,128,128]{2,1,0:T(8,128)(2,1)S(1)}, u32[]{:S(2)}, u32[]{:S(2)}) %all-to-all-start.1) | async-done | bytes 262176 | tf_op jit(solution)/shard_map/all_to_all | solution.py:36
  43.2 0.1 reshape.146
  43.4 0.3 convolution_convert_fusion.1
  43.7 0.2 reshape_reshape.3
  43.9 12.9 %all_to_all.31 = bf16[16,128,128]{2,1,0:T(8,128)(2,1)S(1)} all-to-all(bf16[16,128,128]{2,1,0:T(8,128)(2,1)S(1)} %reshape_reshape.3), channel_id=1, replica_groups=mesh['y'=4,'zq'=8,'zp'=2,'xl'=2,'xh'=2,'c'=2] {'y','zp','xl'}, dimensions={0} | all-to-all | bytes 1048576 | tf_op jit(solution)/shard_map/all_to_all | solution.py:36
  56.8 0.1 copy.24
  56.9 0.3 fusion.2
  57.2 0.1 copy.26
  57.4 8.0 %all-gather.2 = bf16[16,128,128]{2,1,0:T(8,128)(2,1)S(1)} all-gather(bf16[4,128,128]{2,1,0:T(8,128)(2,1)S(1)} %copy.26), channel_id=4, replica_groups=mesh['y'=4,'zq'=8,'zp'=2,'xl'=2,'xh'=2,'c'=2] {'xh','c'}, dimensions={0}, use_global_device_ids=true | all-gather | bytes 655360 | tf_op jit(solution)/shard_map/all_gather | solution.py:141
  65.5 0.5 fusion.10
  66.0 0.2 fusion.3
  66.2 0.2 convolution_convert_fusion.3
  66.4 0.4 convolution_convert_fusion
  66.8 0.1 copy.43
  67.0 15.5 %all_to_all.32 = bf16[16,144,128]{2,1,0:T(8,128)(2,1)S(1)} all-to-all(bf16[16,144,128]{2,1,0:T(8,128)(2,1)S(1)} %maximum_bitcast_fusion), channel_id=1, replica_groups=mesh['y'=4,'zq'=8,'zp'=2,'xl'=2,'xh'=2,'c'=2] {'y','zp','xl'}, dimensions={0} | all-to-all | bytes 1179648 | tf_op jit(solution)/shard_map/all_to_all | solution.py:36
  82.6 0.2 fusion
  82.9 24.4 %all_to_all.33.parts_ref = bf16[8,144,128]{2,1,0:T(8,128)(2,1)S(1)} all-to-all(bf16[8,144,128]{2,1,0:T(8,128)(2,1)S(1)} %maximum_bitcast_fusion.1), channel_id=1, replica_groups={{64,80,96,112,0,16,32,48},{65,81,97,113,1,17,33,49},{66,82,98,114,2,18,..., dimensions={0} | all-to-all | bytes 589824 | tf_op jit(solution)/shard_map/all_to_all | solution.py:36
  107.3 0.7 sum_far.1
  108.0 3.5 %all-to-all-start.5 = ((bf16[16,24,128]{2,1,0:T(8,128)(2,1)}), bf16[16,24,128]{2,1,0:T(8,128)(2,1)S(1)}, u32[]{:S(2)}, u32[]{:S(2)}) async-start(bf16[16,24,128]{2,1,0:T(8,128)(2,1)} %sum_far.1), calls=%async_computation.5 | async-start | bytes 196608 | tf_op jit(solution)/shard_map/all_to_all | solution.py:36
  111.5 0.7 fusion.14
  112.2 6.6 %all-to-all-done.5.parts_ref = bf16[16,24,128]{2,1,0:T(8,128)(2,1)S(1)} async-done(((bf16[16,24,128]{2,1,0:T(8,128)(2,1)}), bf16[16,24,128]{2,1,0:T(8,128)(2,1)S(1)}, u32[]{:S(2)}, u32[]{:S(2)}) %all-to-all-start.5) | async-done | bytes 98336 | tf_op jit(solution)/shard_map/all_to_all | solution.py:36
  118.8 0.7 unpack.1
  (21 shorter events, 0.4 us)
Async XLA Ops:
  0.6 42.6 %copy-start = (bf16[4,1,4,128,128]{4,3,2,1,0:T(8,128)(2,1)S(1)}, bf16[4,1,4,128,128]{4,3,2,1,0:T(8,128)(2,1)}, u32[]{:S(2)}) copy-start(bf16[4,1,4,128,128]{4,3,2,1,0:T(8,128)(2,1)} %param.11) | copy-start | bytes 1572868
  15.1 15.8 %copy-start.2 = (bf16[128,256]{1,0:T(8,128)(2,1)S(1)}, bf16[128,256]{1,0:T(8,128)(2,1)}, u32[]{:S(2)}) copy-start(bf16[128,256]{1,0:T(8,128)(2,1)} %param.8) | copy-start | bytes 196612
  15.1 28.1 %all-to-all-start.1 = ((bf16[8,128,128]{2,1,0:T(8,128)(2,1)}), bf16[8,128,128]{2,1,0:T(8,128)(2,1)S(1)}, u32[]{:S(2)}, u32[]{:S(2)}) async-start(bf16[8,128,128]{2,1,0:T(8,128)(2,1)} %broadcast_in_dim.9), calls=%async_computation.1 | async-start | bytes 524288 | tf_op jit(solution)/shard_map/all_to_all | solution.py:36
  39.8 0.8 copy-start.1
  108.0 10.8 %all-to-all-start.5 = ((bf16[16,24,128]{2,1,0:T(8,128)(2,1)}), bf16[16,24,128]{2,1,0:T(8,128)(2,1)S(1)}, u32[]{:S(2)}, u32[]{:S(2)}) async-start(bf16[16,24,128]{2,1,0:T(8,128)(2,1)} %sum_far.1), calls=%async_computation.5 | async-start | bytes 196608 | tf_op jit(solution)/shard_map/all_to_all | solution.py:36

commit v10 on v9

--- a/solution.py
+++ b/solution.py
@@ -119,7 +119,7 @@
     pick = (codes[:, None] == rows_in(BACK)[None, :]).astype(bf16)
     halves = jnp.stack([upstream[:, :width], upstream[:, width:]])
     first, halves, weight = lax.optimization_barrier((first, halves, weight))
-    upstream_all = lax.all_gather(lax.all_gather(halves, "xh", axis=0), "c", axis=1)
+    upstream_all = lax.all_gather(lax.all_gather(halves, "c", axis=0), "xh", axis=0)
     upstream_all = upstream_all.transpose(0, 1, 3, 2, 4).reshape(blocks * TILE, 2 * width).astype(f32)
     turned = jnp.swapaxes(values, 2, 3)
     weight = pl.pallas_call(

time: 120 us -> 120 us (level)
  no operation moved by 1% of the time
where the time goes in v10:
time: 120 us; the launch traced here: 119 us
  blocking collectives  82.6 us (69%)
  starting transfers between devices  19.3 us (16%)
  waiting for transfers between devices  7.9 us (7%)
  Pallas kernels  2.88 us (2%)
  local copies, waits for them, and re-layouts  2.77 us (2%)
  matrix products  2.16 us (2%)
    all_to_all x4, blocking collectives, exchange(): lax.all_to_all(flat, axes, split_axis=0, concat_axis=0, axis_index_groups...  65 us
    all_to_all x2, starting transfers between devices, exchange(): lax.all_to_all(flat, axes, split_axis=0, concat_axis=0, axis_index_groups...  19.3 us
    all_gather x1, blocking collectives, body(): shared = lax.all_gather(partial_value, REP, axis=0)  8.02 us
    all_to_all x2, waiting for transfers between devices, exchange(): lax.all_to_all(flat, axes, split_axis=0, concat_axis=0, axis_index_groups...  7.9 us
    all_gather x1, blocking collectives, body(): lax.all_gather(lax.all_gather(halves, 'c', axis=0), 'xh', axis=0)  7.73 us
  transfers between devices with their start and end apart: 2, of which 2 were waited for; matrix products, arithmetic and copies ran while one was open for 1% of the time, Pallas kernels for 0%

profile of v10, /device:TPU:4, one launch (start us, length us, event | category | flops | bytes accessed | tf_op | source)
XLA Modules:
  0.0 119.5 jit_solution(1848184144636956429)
XLA Ops:
  0.6 1.5 %start.1 = bf16[16,16,128]{2,1,0:T(8,128)(2,1)} custom-call(bf16[128,128]{1,0:T(8,128)(2,1)} %features_in.1, s32[4,4]{1,0:T(4,128)} %bitcast.93, s32[1,4]{1,0:T(1,128)} %bitcast.94), custom_call_target="tpu_custom_call" | custom-call | tf_op jit(solution)/shard_map/start/pallas_call | solution.py:102
  2.2 12.2 %all_to_all.30 = bf16[16,16,128]{2,1,0:T(8,128)(2,1)S(1)} all-to-all(bf16[16,16,128]{2,1,0:T(8,128)(2,1)} %start.1), channel_id=1, replica_groups={{256,260,264,268,384,388,392,396,0,4,8,12,128,132,136,140},{257,261,265..., dimensions={0} | all-to-all | bytes 131072 | tf_op jit(solution)/shard_map/all_to_all | solution.py:36
  14.3 0.7 broadcast_in_dim.9
  15.1 15.8 %all-to-all-start.1 = ((bf16[8,128,128]{2,1,0:T(8,128)(2,1)}), bf16[8,128,128]{2,1,0:T(8,128)(2,1)S(1)}, u32[]{:S(2)}, u32[]{:S(2)}) async-start(bf16[8,128,128]{2,1,0:T(8,128)(2,1)} %broadcast_in_dim.9), calls=%async_computation.1 | async-start | bytes 524288 | tf_op jit(solution)/shard_map/all_to_all | solution.py:36
  30.9 1.9 %all-gather = bf16[4,128,128]{2,1,0:T(8,128)(2,1)S(1)} all-gather(bf16[2,128,128]{2,1,0:T(8,128)(2,1)S(1)} %pad_maximum_fusion.1), channel_id=2, replica_groups=mesh['y'=4,'zq'=8,'zp'=2,'xl'=2,'xh'=2,'c'=2] {'c'}, dimensions={0}, use_global_device_ids=true | all-gather | bytes 196608 | tf_op jit(solution)/shard_map/all_gather | solution.py:122
  32.8 7.7 %all-gather.1 = bf16[4,2,128,128]{3,2,1,0:T(8,128)(2,1)S(1)} all-gather(bf16[2,2,128,128]{3,2,1,0:T(8,128)(2,1)S(1)} %bitcast.91), channel_id=3, replica_groups=mesh['y'=4,'zq'=8,'zp'=2,'xl'=2,'xh'=2,'c'=2] {'xh'}, dimensions={0}, use_global_device_ids=true | all-gather | bytes 393216 | tf_op jit(solution)/shard_map/all_gather | solution.py:122
  40.6 0.3 copy.24
  40.9 0.8 copy-done.1
  41.7 0.1 reshape.158
  41.8 0.1 compare_convert_fusion
  41.9 1.3 %all-to-all-done.1 = bf16[8,128,128]{2,1,0:T(8,128)(2,1)S(1)} async-done(((bf16[8,128,128]{2,1,0:T(8,128)(2,1)}), bf16[8,128,128]{2,1,0:T(8,128)(2,1)S(1)}, u32[]{:S(2)}, u32[]{:S(2)}) %all-to-all-start.1) | async-done | bytes 262176 | tf_op jit(solution)/shard_map/all_to_all | solution.py:36
  43.2 0.1 reshape.146
  43.4 0.3 convolution_convert_fusion.1
  43.7 0.2 reshape_reshape.3
  43.9 12.9 %all_to_all.31 = bf16[16,128,128]{2,1,0:T(8,128)(2,1)S(1)} all-to-all(bf16[16,128,128]{2,1,0:T(8,128)(2,1)S(1)} %reshape_reshape.3), channel_id=1, replica_groups=mesh['y'=4,'zq'=8,'zp'=2,'xl'=2,'xh'=2,'c'=2] {'y','zp','xl'}, dimensions={0} | all-to-all | bytes 1048576 | tf_op jit(solution)/shard_map/all_to_all | solution.py:36
  56.8 0.1 copy.25
  56.9 0.3 fusion.2
  57.2 0.1 copy.27
  57.4 8.0 %all-gather.2 = bf16[16,128,128]{2,1,0:T(8,128)(2,1)S(1)} all-gather(bf16[4,128,128]{2,1,0:T(8,128)(2,1)S(1)} %copy.27), channel_id=4, replica_groups=mesh['y'=4,'zq'=8,'zp'=2,'xl'=2,'xh'=2,'c'=2] {'xh','c'}, dimensions={0}, use_global_device_ids=true | all-gather | bytes 655360 | tf_op jit(solution)/shard_map/all_gather | solution.py:141
  65.5 0.5 fusion.10
  66.0 0.2 fusion.3
  66.2 0.2 convolution_convert_fusion.3
  66.4 0.4 convolution_convert_fusion
  66.8 0.1 copy.44
  67.0 15.5 %all_to_all.32 = bf16[16,144,128]{2,1,0:T(8,128)(2,1)S(1)} all-to-all(bf16[16,144,128]{2,1,0:T(8,128)(2,1)S(1)} %maximum_bitcast_fusion), channel_id=1, replica_groups=mesh['y'=4,'zq'=8,'zp'=2,'xl'=2,'xh'=2,'c'=2] {'y','zp','xl'}, dimensions={0} | all-to-all | bytes 1179648 | tf_op jit(solution)/shard_map/all_to_all | solution.py:36
  82.6 0.2 fusion
  82.9 24.4 %all_to_all.33.parts_ref = bf16[8,144,128]{2,1,0:T(8,128)(2,1)S(1)} all-to-all(bf16[8,144,128]{2,1,0:T(8,128)(2,1)S(1)} %maximum_bitcast_fusion.1), channel_id=1, replica_groups={{64,80,96,112,0,16,32,48},{65,81,97,113,1,17,33,49},{66,82,98,114,2,18,..., dimensions={0} | all-to-all | bytes 589824 | tf_op jit(solution)/shard_map/all_to_all | solution.py:36
  107.3 0.7 sum_far.1
  108.0 3.5 %all-to-all-start.5 = ((bf16[16,24,128]{2,1,0:T(8,128)(2,1)}), bf16[16,24,128]{2,1,0:T(8,128)(2,1)S(1)}, u32[]{:S(2)}, u32[]{:S(2)}) async-start(bf16[16,24,128]{2,1,0:T(8,128)(2,1)} %sum_far.1), calls=%async_computation.5 | async-start | bytes 196608 | tf_op jit(solution)/shard_map/all_to_all | solution.py:36
  111.5 0.7 fusion.14
  112.2 6.6 %all-to-all-done.5.parts_ref = bf16[16,24,128]{2,1,0:T(8,128)(2,1)S(1)} async-done(((bf16[16,24,128]{2,1,0:T(8,128)(2,1)}), bf16[16,24,128]{2,1,0:T(8,128)(2,1)S(1)}, u32[]{:S(2)}, u32[]{:S(2)}) %all-to-all-start.5) | async-done | bytes 98336 | tf_op jit(solution)/shard_map/all_to_all | solution.py:36
  118.8 0.7 unpack.1
  (20 shorter events, 0.4 us)
Async XLA Ops:
  0.6 42.6 %copy-start = (bf16[4,1,4,128,128]{4,3,2,1,0:T(8,128)(2,1)S(1)}, bf16[4,1,4,128,128]{4,3,2,1,0:T(8,128)(2,1)}, u32[]{:S(2)}) copy-start(bf16[4,1,4,128,128]{4,3,2,1,0:T(8,128)(2,1)} %param.11) | copy-start | bytes 1572868
  15.1 15.8 %copy-start.2 = (bf16[128,256]{1,0:T(8,128)(2,1)S(1)}, bf16[128,256]{1,0:T(8,128)(2,1)}, u32[]{:S(2)}) copy-start(bf16[128,256]{1,0:T(8,128)(2,1)} %param.8) | copy-start | bytes 196612
  15.1 28.1 %all-to-all-start.1 = ((bf16[8,128,128]{2,1,0:T(8,128)(2,1)}), bf16[8,128,128]{2,1,0:T(8,128)(2,1)S(1)}, u32[]{:S(2)}, u32[]{:S(2)}) async-start(bf16[8,128,128]{2,1,0:T(8,128)(2,1)} %broadcast_in_dim.9), calls=%async_computation.1 | async-start | bytes 524288 | tf_op jit(solution)/shard_map/all_to_all | solution.py:36
  40.8 0.8 copy-start.1
  108.0 10.8 %all-to-all-start.5 = ((bf16[16,24,128]{2,1,0:T(8,128)(2,1)}), bf16[16,24,128]{2,1,0:T(8,128)(2,1)S(1)}, u32[]{:S(2)}, u32[]{:S(2)}) async-start(bf16[16,24,128]{2,1,0:T(8,128)(2,1)} %sum_far.1), calls=%async_computation.5 | async-start | bytes 196608 | tf_op jit(solution)/shard_map/all_to_all | solution.py:36
